TPU v7x, 512 devices: a whole 4x4x16 slice. The times are simulated.
512 devices in a mesh: gx: 8 (over x, core), gy: 4 (over y), gz: 16 (over z).
Axes of the slice: x: 4, y: 4, z: 16, core: 2. Of those that a mesh axis runs over, the one named last changes fastest.
Arguments:
- flow_state: float32 [8, 4, 16, 5, 4, 128, 128], P('gx', 'gy', 'gz'), may hold values from -2 to 8, as said below
- face_links: int32 [8, 4, 16, 4], P('gx', 'gy', 'gz'), may hold values from 0 to 15, as said below
- donor_plane: int32 [8, 4, 16, 64], P('gx', 'gy', 'gz'), may hold values from 0 to 2
- donor_line: int32 [8, 4, 16, 64], P('gx', 'gy', 'gz'), may hold values from 0 to 126
- donor_weights: float32 [8, 4, 16, 64, 3], P('gx', 'gy', 'gz'), may hold values from 0 to 1
- receptor_owner: int32 [8, 4, 16, 64, 1], P('gx', 'gy', 'gz'), may hold values from 0 to 63; in each aligned block of 64 rows (0 to 63, 64 to 127, ..., all dimensions but the last counted through in order) at most 2 rows name the same one
Outputs:
- new_state: float32 [8, 4, 16, 5, 4, 128, 128], P('gx', 'gy', 'gz')
- fringe: float32 [8, 4, 16, 128, 640], P('gx', 'gy', 'gz')
Inputs may be any that keep to these rules, and one draw needn't show every extreme that they name: `flow_state`: the state of every cell has density in [0.5, 2], velocity components in [-1, 1] and pressure in [0.5, 2]. face_links holds indices along the third block index within the same column of blocks and flags 0 or 1; in each column the k-high links form one closed loop through all 16 blocks, and a block's k-high neighbour has that block as its k-low neighbour with the same flag. `receptor_owner`: among the donor lines of one block no owner is named more than 2 times, a bound that some block reaches.
All inputs are finite; a program needn't handle non-finite values.
Results may differ from a plain program's by a relative error of at most 0.000071.
Values sent between devices are 32-bit elements; how exact they have to be, the bound alone decides.
A program may use at most 128 MiB of HBM per device.

v0:
```python
import jax
import jax.numpy as jnp
from jax import lax
from jax.sharding import PartitionSpec as P

GAMMA = 1.4
DT_DX = 0.08


def cell_fluxes(values, direction):
    density = values[0]
    momentum = values[1:4]
    energy = values[4]
    velocity = momentum / density
    pressure = (GAMMA - 1.0) * (energy - 0.5 * jnp.sum(momentum * velocity, axis=0))
    sound_speed = jnp.sqrt(GAMMA * pressure / density)
    normal_speed = velocity[direction]
    pieces = [momentum[direction]]
    for component in range(3):
        term = momentum[component] * normal_speed
        if component == direction:
            term = term + pressure
        pieces.append(term)
    pieces.append((energy + pressure) * normal_speed)
    return (jnp.stack(pieces), jnp.abs(normal_speed) + sound_speed)


def edge_pad(values, axis_index):
    count = values.shape[axis_index]
    first = lax.slice_in_dim(values, 0, 1, axis=axis_index)
    last = lax.slice_in_dim(values, count - 1, count, axis=axis_index)
    return jnp.concatenate([first, values, last], axis=axis_index)


def face_flux(padded, direction):
    axis_index = direction + 1
    count = padded.shape[axis_index]
    cell_flux, speed = cell_fluxes(padded, direction)
    left_flux = lax.slice_in_dim(cell_flux, 0, count - 1, axis=axis_index)
    right_flux = lax.slice_in_dim(cell_flux, 1, count, axis=axis_index)
    left_speed = lax.slice_in_dim(speed, 0, count - 1, axis=direction)
    right_speed = lax.slice_in_dim(speed, 1, count, axis=direction)
    left_state = lax.slice_in_dim(padded, 0, count - 1, axis=axis_index)
    right_state = lax.slice_in_dim(padded, 1, count, axis=axis_index)
    return 0.5 * (left_flux + right_flux) - 0.5 * jnp.maximum(left_speed, right_speed) * (
        right_state - left_state
    )


def difference(faces_flux, axis_index):
    count = faces_flux.shape[axis_index]
    return lax.slice_in_dim(faces_flux, 1, count, axis=axis_index) - lax.slice_in_dim(
        faces_flux, 0, count - 1, axis=axis_index
    )


def interpolate(extended, donor_plane, donor_line, donor_weights):
    count = extended.shape[3] - 2
    plane_frac = donor_weights[:, 0][:, None, None]
    line_frac = donor_weights[:, 1][:, None, None]
    cell_frac = donor_weights[:, 2][:, None, None]
    summed = jnp.zeros((donor_plane.shape[0], extended.shape[0], count), jnp.float32)
    for plane_step in range(2):
        plane_weight = plane_frac if plane_step == 1 else 1.0 - plane_frac
        for line_step in range(2):
            line_weight = line_frac if line_step == 1 else 1.0 - line_frac
            picked = extended[:, donor_plane + plane_step, donor_line + line_step, :]
            picked = jnp.transpose(picked, (1, 0, 2))
            inner = (1.0 - cell_frac) * picked[:, :, 1 : count + 1] + cell_frac * picked[
                :, :, 2 : count + 2
            ]
            summed = summed + plane_weight * line_weight * inner
    return summed


def flip_where(layer, flag):
    return jnp.where(flag == 1, jnp.flip(layer, -1), layer)


def local(flow_state, face_links, donor_plane, donor_line, donor_weights, receptor_owner):
    local_block = flow_state[0, 0, 0]
    link_table = face_links[0, 0, 0]
    first_layer = local_block[..., 0]
    last_layer = local_block[..., -1]
    face_pair = jnp.stack([first_layer, last_layer])
    gathered = lax.all_gather(face_pair[None], "gz", axis=0, tiled=True)
    low_source = lax.dynamic_index_in_dim(gathered, link_table[0], 0, keepdims=False)
    high_source = lax.dynamic_index_in_dim(gathered, link_table[2], 0, keepdims=False)
    low_ghost = flip_where(low_source[1], link_table[1])
    high_ghost = flip_where(high_source[0], link_table[3])
    extended = jnp.concatenate([low_ghost[..., None], local_block, high_ghost[..., None]], axis=3)
    row_values = interpolate(
        extended, donor_plane[0, 0, 0], donor_line[0, 0, 0], donor_weights[0, 0, 0]
    )
    row_count = row_values.shape[0]
    row_values = row_values.reshape(row_count, -1)
    group_size = lax.axis_size("gy") * lax.axis_size("gz")
    capacity = max(2, 2 * row_count // group_size)
    owner_ids = receptor_owner[0, 0, 0, :, 0]
    onehot = (owner_ids[:, None] == jnp.arange(group_size, dtype=jnp.int32)[None, :]).astype(
        jnp.int32
    )
    earlier = jnp.cumsum(onehot, axis=0) - onehot
    rank_order = jnp.sum(onehot * earlier, axis=1)
    slot_index = owner_ids * capacity + rank_order
    selector = (
        jnp.arange(group_size * capacity, dtype=jnp.int32)[:, None] == slot_index[None, :]
    ).astype(jnp.float32)
    outgoing_rows = jnp.dot(
        selector, row_values, precision=lax.Precision.HIGHEST, preferred_element_type=jnp.float32
    )
    change = difference(face_flux(edge_pad(local_block, 1), 0), 1)
    change = change + difference(face_flux(edge_pad(local_block, 2), 1), 2)
    change = change + difference(face_flux(extended, 2), 3)
    new_state = local_block - DT_DX * change
    packed = outgoing_rows.reshape(group_size, capacity, -1)
    arrived = lax.all_to_all(packed, ("gy", "gz"), split_axis=0, concat_axis=0, tiled=True)
    fringe = arrived.reshape(1, 1, 1, group_size * capacity, -1)
    return (new_state[None, None, None], fringe)


def solution(mesh):
    return jax.shard_map(
        local,
        mesh=mesh,
        in_specs=(
            P("gx", "gy", "gz", None, None, None, None),
            P("gx", "gy", "gz", None),
            P("gx", "gy", "gz", None),
            P("gx", "gy", "gz", None),
            P("gx", "gy", "gz", None, None),
            P("gx", "gy", "gz", None, None),
        ),
        out_specs=(P("gx", "gy", "gz", None, None, None, None), P("gx", "gy", "gz", None, None)),
        check_vma=False,
    )
```

profile of v0, /device:TPU:2, one launch (start us, length us, event | category | flops | bytes accessed | tf_op | source)
XLA Modules:
  0.0 119.3 jit_solution(4250096986131630276)
XLA Ops:
  0.6 1.4 %fusion.65 = (s32[1,1,1,1]{3,2,1,0:T(1,128)}, s32[1,1,1,1]{3,2,1,0:T(1,128)}, s32[1,1,1,1]{3,2,1,0:T(1,128)}, s32[1,1,1,1]{3,2,1,0:T(1,128)}) fusion(s32[1,1,1,4]{3,2,1,0:T(1,128)} %param.7), kind=kLoop, calls=%fused_computation.156 | loop fusion | bytes 32 | tf_op jit(solution)/shard_map/slice | solution.py:89
  4.5 0.7 copy.353
  5.2 2.2 %copy.351 = f32[1,1,1,5,4,128,128]{6,4,5,3,2,1,0:T(4,128)S(1)} copy(f32[1,1,1,5,4,128,128]{6,5,4,3,2,1,0:T(8,128)} %param.6) | data formatting | bytes 2621440 | tf_op args[0]
  7.3 1.8 %fusion.64 = (f32[5,4,128,1]{3,1,2,0:T(4,128)S(1)}, f32[5,4,128,1]{3,1,2,0:T(4,128)}) fusion(f32[5,4,128,128]{3,1,2,0:T(4,128)S(1)} %bitcast.150), kind=kLoop, calls=%fused_computation.155 | loop fusion | bytes 40960 | tf_op jit(solution)/shard_map/slice | solution.py:83
  9.1 1.7 %copy.292 = f32[5,4,128,1]{2,1,0,3:T(4,128)S(1)} copy(f32[5,4,128,1]{3,1,2,0:T(4,128)} %get-tuple-element.38) | data formatting | bytes 20480 | tf_op jit(solution)/shard_map/slice | solution.py:84
  10.8 0.4 copy.291
  11.3 37.2 %all-gather = f32[32,5,4,128]{3,2,1,0:T(4,128)S(1)} all-gather(f32[2,5,4,128]{3,2,1,0:T(4,128)S(1)} %pad_maximum_fusion.3), channel_id=2, replica_groups=mesh['gx'=8,'gy'=4,'gz'=16] {'gz'}, dimensions={0}, use_global_device_ids=true | all-gather | bytes 348160 | tf_op jit(solution)/shard_map/all_gather | solution.py:86
  49.8 0.1 rev.8
  49.9 0.1 rev.7
  51.3 0.5 copy.294
  51.8 1.5 %copy.293 = f32[5,4,128,1]{3,1,2,0:T(4,128)} copy(f32[5,4,128,1]{2,1,0,3:T(4,128)S(1)} %get-tuple-element.55) | data formatting | bytes 20480 | tf_op jit(solution)/shard_map/broadcast_in_dim | solution.py:91
  53.3 3.4 %pad_maximum_fusion.1 = f32[5,4,128,130]{3,1,2,0:T(4,128)S(1)} fusion(f32[5,4,128,1]{3,1,2,0:T(4,128)S(1)} %copy.294, f32[5,4,128,128]{3,1,2,0:T(4,128)S(1)} %bitcast.151, f32[5,4,128,1]{3,1,2,0:T(4,128)} %copy.293), kind=kLoop, calls=%fused_computation.13 | loop fusion | flops 665600 | bytes 2662400 | tf_op jit(solution)/shard_map/concatenate | solution.py:91
  56.7 3.6 %copy.308 = f32[5,4,128,130]{3,0,2,1:T(8,128)} copy(f32[5,4,128,130]{3,1,2,0:T(4,128)S(1)} %pad_maximum_fusion.1) | data formatting | bytes 2662400 | tf_op jit(solution)/shard_map/concatenate | solution.py:91
  60.3 2.9 %gather_fusion.3 = f32[64,5,130]{2,1,0:T(8,128)S(1)} fusion(f32[5,4,128,130]{3,0,2,1:T(8,128)} %copy.308, s32[64]{0:T(128)S(1)} %get-tuple-element.47), kind=kCustom, calls=%fused_computation.3 | custom fusion | bytes 333312 | tf_op jit(solution)/shard_map/gather | solution.py:67
  63.2 3.7 %gather_fusion.2 = f32[64,5,130]{2,1,0:T(8,128)} fusion(f32[5,4,128,130]{3,0,2,1:T(8,128)} %copy.308, s32[64]{0:T(128)S(1)} %get-tuple-element.48), kind=kCustom, calls=%fused_computation.2 | custom fusion | bytes 333312 | tf_op jit(solution)/shard_map/gather | solution.py:67
  66.9 3.7 %gather_fusion.1 = f32[64,5,130]{2,1,0:T(8,128)} fusion(f32[5,4,128,130]{3,0,2,1:T(8,128)} %copy.308, s32[64]{0:T(128)S(1)} %get-tuple-element.49), kind=kCustom, calls=%fused_computation.1 | custom fusion | bytes 333312 | tf_op jit(solution)/shard_map/gather | solution.py:67
  70.6 3.7 %gather_fusion = f32[64,5,130]{2,1,0:T(8,128)} fusion(f32[5,4,128,130]{3,0,2,1:T(8,128)} %copy.308, s32[64]{0:T(128)S(1)} %get-tuple-element.46), kind=kCustom, calls=%fused_computation | custom fusion | bytes 333312 | tf_op jit(solution)/shard_map/gather | solution.py:67
  74.3 2.9 %fusion.38 = f32[64,5,128]{2,1,0:T(8,128)S(1)} fusion(f32[64,5,130]{2,1,0:T(8,128)S(1)} %gather_fusion.3, f32[64,5,130]{2,1,0:T(8,128)} %gather_fusion.2, f32[64,5,130]{2,1,0:T(8,128)} %gather_fusion.1, f32[64,5,130]{2,1,0:T(8,128)} %gather_fusion, f32[64]{0:T(128)S(1)} %get-tuple-element.45, f32[64]{0:T(128)S(1)} %get-tuple-element.44, ...), kind=kLoop, calls=%fused_computation.92 | loop fusion | flops 778240 | bytes 1476096 | tf_op jit(solution)/shard_map/add | solution.py:72
  77.3 0.1 fusion.50
  77.3 0.1 reduce_window_sum.11
  77.4 0.2 select_reduce_fusion
  77.6 0.3 fusion.47
  78.0 1.0 copy.312
  78.9 10.7 %all-to-all-start = ((f32[64,2,640]{2,1,0:T(2,128)}), f32[64,2,640]{2,1,0:T(2,128)}, u32[]{:S(2)}, u32[]{:S(2)}) async-start(f32[64,2,640]{2,1,0:T(2,128)} %copy.312), calls=%async_computation | async-start | bytes 655360 | tf_op jit(solution)/shard_map/all_to_all | solution.py:117
  89.7 2.6 %slice_bitcast_fusion.1 = (f32[4,128,130]{2,0,1:T(4,128)}, f32[5,4,128,130]{3,1,2,0:T(4,128)}, f32[1,4,128,130]{3,1,2,0:T(4,128)S(1)}) fusion(f32[5,4,128,130]{3,1,2,0:T(4,128)} %copy-done), kind=kLoop, calls=%fused_computation.73 | loop fusion | bytes 2113536 | tf_op jit(solution)/shard_map/squeeze | solution.py:13
  92.3 1.2 %fusion.62 = (f32[5,1,128,128]{3,1,2,0:T(1,128)S(1)}, f32[5,1,128,128]{3,1,2,0:T(1,128)}) fusion(f32[5,4,128,128]{3,1,2,0:T(4,128)S(1)} %bitcast.153), kind=kLoop, calls=%fused_computation.153 | loop fusion | bytes 1310720 | tf_op jit(solution)/shard_map/slice | solution.py:30
  93.5 0.9 copy.295
  94.5 2.0 %copy.296 = f32[4,128,130]{2,0,1:T(4,128)} copy(f32[4,128,130]{1,2,0:T(8,128)} %bitcast.161) | data formatting | bytes 532480 | tf_op jit(solution)/shard_map/div | solution.py:14
  96.4 2.4 %multiply_reduce_fusion = (f32[4,128,130]{2,0,1:T(4,128)S(1)}, f32[3,4,128,130]{3,1,2,0:T(4,128)S(1)}) fusion(f32[5,4,128,130]{3,1,2,0:T(4,128)} %copy-done, f32[4,128,130]{2,0,1:T(4,128)} %copy.296), kind=kLoop, calls=%fused_computation.16 | loop fusion | flops 532480 | bytes 2129920 | tf_op jit(solution)/shard_map/reduce_sum | solution.py:15
  98.9 0.9 fusion.16
  99.8 0.9 fusion.15
  100.8 0.1 fusion.29
  100.9 1.5 %abs_bitcast_fusion = (f32[4,128,130]{2,0,1:T(4,128)S(1)}, f32[5,4,128,130]{3,1,2,0:T(4,128)}) fusion(f32[3,4,128,130]{3,1,2,0:T(4,128)S(1)} %get-tuple-element.23, f32[5,4,128,130]{3,1,2,0:T(4,128)} %fusion.15, f32[1,4,128,130]{3,2,1,0:T(8,128)S(1)} %fusion.29, f32[5,4,128,130]{3,1,2,0:T(4,128)S(1)} %copy-done.1), kind=kLoop, calls=%fused_computation.65 | loop fusion | flops 332800 | bytes 1855488 | tf_op jit(solution)/shard_map/abs | solution.py:25
  102.4 0.4 fusion.21
  102.8 0.2 fusion.14
  103.0 0.3 copy.305
  103.4 0.3 pad_maximum_fusion.2
  103.8 0.1 copy.283
  103.8 0.3 multiply_reduce_fusion.2
  104.1 0.1 fusion.31
  104.2 0.3 bitcast_add_fusion
  104.5 0.2 add_dynamic-update-slice_fusion.2
  104.7 0.1 fusion.30
  104.8 0.2 multiply_dynamic-update-slice_fusion.2
  105.0 0.1 fusion.35
  105.0 0.6 copy-done.5
  105.7 0.8 pad_maximum_fusion
  106.5 0.1 slice_bitcast_fusion
  106.6 0.3 multiply_reduce_fusion.1
  106.9 0.2 fusion.27
  107.1 0.2 add_dynamic-update-slice_fusion.1
  107.3 0.1 fusion.19
  107.3 0.1 fusion.18
  107.4 0.1 multiply_dynamic-update-slice_fusion.1
  107.5 0.1 fusion.17
  107.6 0.5 fusion.7
  108.2 1.5 %fusion.3 = f32[5,5,128,128]{3,1,2,0:T(8,128)S(1)} fusion(f32[5,6,128,128]{3,1,2,0:T(8,128)S(1)} %multiply_dynamic-update-slice_fusion.1, f32[5,1,128,128]{3,1,2,0:T(1,128)S(1)} %copy-done.5, f32[5,4,128,128]{3,1,2,0:T(4,128)S(1)} %bitcast.157, f32[5,1,128,128]{3,1,2,0:T(1,128)S(1)} %get-tuple-element.33, f32[5,128,128]{2,0,1:T(8,128)S(1)} %fusion.17), kind=kLoop, calls=%fused_computation.9 | loop fusion | flops 2867200 | bytes 7208960 | tf_op jit(solution)/shard_map/sub | solution.py:45
  109.6 0.3 copy-done.2
  109.9 0.6 multiply_dynamic-update-slice_fusion
  110.4 0.6 copy-done.3
  111.0 3.0 %fusion.1 = f32[5,4,128,129]{3,1,2,0:T(4,128)S(1)} fusion(f32[5,4,128,130]{3,1,2,0:T(4,128)S(1)} %multiply_dynamic-update-slice_fusion, f32[5,4,128,1]{3,1,2,0:T(4,128)S(1)} %copy.294, f32[5,4,128,128]{3,1,2,0:T(4,128)S(1)} %bitcast.158, f32[5,4,128,1]{3,1,2,0:T(4,128)S(1)} %copy-done.3, f32[4,128,129]{2,0,1:T(4,128)S(1)} %copy.305), kind=kLoop, calls=%fused_computation.6 | loop fusion | flops 2311680 | bytes 5558272 | tf_op jit(solution)/shard_map/sub | solution.py:45
  114.1 2.1 %fusion.12 = f32[1,1,1,5,4,128,128]{6,4,5,3,2,1,0:T(4,128)S(1)} fusion(f32[5,4,128,129]{3,1,2,0:T(4,128)S(1)} %fusion.1, f32[5,4,129,128]{3,1,2,0:T(4,128)S(1)} %fusion.7, f32[5,5,128,128]{3,1,2,0:T(8,128)S(1)} %fusion.3, f32[1,1,1,5,4,128,128]{6,5,4,3,2,1,0:T(8,128)S(1)} %copy-done.4), kind=kLoop, calls=%fused_computation.30 | loop fusion | flops 2293760 | bytes 10485760 | tf_op jit(solution)/shard_map/broadcast_in_dim | solution.py:119
  116.2 1.2 %copy.313 = f32[1,1,1,5,4,128,128]{6,5,4,3,2,1,0:T(8,128)} copy(f32[1,1,1,5,4,128,128]{6,4,5,3,2,1,0:T(4,128)S(1)} %fusion.12) | data formatting | bytes 2621440
  117.4 1.9 %reshape.253 = f32[1,1,1,128,640]{4,3,2,1,0:T(8,128)} reshape(f32[64,2,640]{2,1,0:T(2,128)} %all-to-all-done) | data formatting | bytes 655360 | tf_op jit(solution)/shard_map/reshape | solution.py:118
  (30 shorter events, 0.2 us)
Async XLA Ops:
  56.7 3.6 %copy-start = (f32[5,4,128,130]{3,1,2,0:T(4,128)}, f32[5,4,128,130]{3,1,2,0:T(4,128)S(1)}, u32[]{:S(2)}) copy-start(f32[5,4,128,130]{3,1,2,0:T(4,128)S(1)} %pad_maximum_fusion.1) | copy-start | bytes 3993604
  56.7 3.6 %copy-start.8 = (s32[1,1,1,64]{3,2,1,0:T(1,128)S(1)}, s32[1,1,1,64]{3,2,1,0:T(1,128)}, u32[]{:S(2)}) copy-start(s32[1,1,1,64]{3,2,1,0:T(1,128)} %param.9) | copy-start | bytes 772
  56.7 3.6 %copy-start.9 = (s32[1,1,1,64]{3,2,1,0:T(1,128)S(1)}, s32[1,1,1,64]{3,2,1,0:T(1,128)}, u32[]{:S(2)}) copy-start(s32[1,1,1,64]{3,2,1,0:T(1,128)} %param.8) | copy-start | bytes 772
  70.6 6.7 %copy-start.7 = (s32[1,1,1,64,1]{3,4,2,1,0:T(1,128)S(1)}, s32[1,1,1,64,1]{3,4,2,1,0:T(1,128)}, u32[]{:S(2)}) copy-start(s32[1,1,1,64,1]{3,4,2,1,0:T(1,128)} %param.11) | copy-start | bytes 772
  78.9 38.4 %all-to-all-start = ((f32[64,2,640]{2,1,0:T(2,128)}), f32[64,2,640]{2,1,0:T(2,128)}, u32[]{:S(2)}, u32[]{:S(2)}) async-start(f32[64,2,640]{2,1,0:T(2,128)} %copy.312), calls=%async_computation | async-start | bytes 655360 | tf_op jit(solution)/shard_map/all_to_all | solution.py:117
  96.4 2.5 %copy-start.1 = (f32[5,4,128,130]{3,1,2,0:T(4,128)S(1)}, f32[5,4,128,130]{3,1,2,0:T(4,128)}, u32[]{:S(2)}) copy-start(f32[5,4,128,130]{3,1,2,0:T(4,128)} %copy-done) | copy-start | bytes 3993604
  100.9 1.5 %copy-start.6 = (f32[4,128,130]{2,0,1:T(4,128)S(1)}, f32[4,128,130]{2,0,1:T(4,128)}, u32[]{:S(2)}) copy-start(f32[4,128,130]{2,0,1:T(4,128)} %get-tuple-element.26) | copy-start | bytes 798724
  104.7 1.0 copy-start.5
  108.1 1.7 %copy-start.2 = (f32[5,4,128,130]{3,1,2,0:T(4,128)S(1)}, f32[5,4,128,130]{3,1,2,0:T(4,128)}, u32[]{:S(2)}) copy-start(f32[5,4,128,130]{3,1,2,0:T(4,128)} %get-tuple-element.30) | copy-start | bytes 3993604
  109.6 1.4 %copy-start.3 = (f32[5,4,128,1]{3,1,2,0:T(4,128)S(1)}, f32[5,4,128,1]{3,1,2,0:T(4,128)}, u32[]{:S(2)}) copy-start(f32[5,4,128,1]{3,1,2,0:T(4,128)} %copy.293) | copy-start | bytes 30724
  111.0 3.1 %copy-start.4 = (f32[1,1,1,5,4,128,128]{6,5,4,3,2,1,0:T(8,128)S(1)}, f32[1,1,1,5,4,128,128]{6,5,4,3,2,1,0:T(8,128)}, u32[]{:S(2)}) copy-start(f32[1,1,1,5,4,128,128]{6,5,4,3,2,1,0:T(8,128)} %param.6) | copy-start | bytes 3932164
where the time goes:
time: 120 us; the launch traced here: 119 us
  local copies, waits for them, and re-layouts  40.9 us (34%)
  blocking collectives  37.2 us (31%)
  other arithmetic  24.2 us (20%)
  starting transfers between devices  10.7 us (9%)
  between operations  5.89 us (5%)
    all_gather x1, blocking collectives, local(): gathered = lax.all_gather(face_pair[None], 'gz', axis=0, tiled=True)  37.2 us
    gather x4, local copies, waits for them, and re-layouts, interpolate(): picked = extended[:, donor_plane + plane_step, donor_line + line_step, :]  14 us
    all_to_all x1, starting transfers between devices, local(): lax.all_to_all(packed, ('gy', 'gz'), split_axis=0, concat_axis=0, tiled=T...  10.7 us
    unnamed x23, local copies, waits for them, and re-layouts  5.56 us
    sub x3, other arithmetic, face_flux(): 0.5 * (left_flux + right_flux)  5.03 us
    concatenate x1, local copies, waits for them, and re-layouts, local(): jnp.concatenate([low_ghost[..., None], local_block, high_ghost[..., None]...  3.57 us
    concatenate x1, other arithmetic, local(): jnp.concatenate([low_ghost[..., None], local_block, high_ghost[..., None]...  3.4 us
    reduce_sum x3, other arithmetic, cell_fluxes(): jnp.sum(momentum * velocity, axis=0)  3.02 us
  transfers between devices with their start and end apart: 1, of which 0 were waited for; matrix products, arithmetic and copies ran while one was open for 22% of the time, Pallas kernels for 0%

commit v1 on v0

v1 whole, which is shorter than its diff:
```python
import jax
import jax.numpy as jnp
from jax import lax
from jax.experimental import pallas as pl
from jax.experimental.pallas import tpu as pltpu
from jax.sharding import PartitionSpec as P

MESH = pl.DeviceIdType.MESH
EXACT = lax.Precision.HIGHEST
NY, NZ, QUAD = 4, 16, 4
GROUP, CAP = 64, 2
VARS, PL, NJ, NK = 5, 4, 128, 128
LINES = 64
PAD = 8
WIDE = VARS * NK
FACE_ROWS = 24
F32 = jnp.float32


def iota(shape, dim):
    return lax.broadcasted_iota(jnp.int32, shape, dim)


def prims(u):
    r = 1.0 / u[0]
    vel = [u[1] * r, u[2] * r, u[3] * r]
    kinetic = u[1] * vel[0] + u[2] * vel[1] + u[3] * vel[2]
    p = 0.4 * (u[4] - 0.5 * kinetic)
    return vel, p, jnp.sqrt(1.4 * p * r)


def flux(u, prim, d):
    vel, p, cs = prim
    n = vel[d]
    f = [u[1 + d]]
    for c in range(3):
        t = u[1 + c] * n
        f.append(t + p if c == d else t)
    f.append((u[4] + p) * n)
    return f, jnp.abs(n) + cs


def face(left, right):
    (ul, fl, sl), (ur, fr, sr) = left, right
    a = jnp.maximum(sl, sr)
    return [0.5 * (fl[v] + fr[v]) - 0.5 * a * (ur[v] - ul[v]) for v in range(VARS)]


def side(u, d):
    f, s = flux(u, prims(u), d)
    return u, f, s


def slot_matrix(dplane, dline, weights, owner):
    own_col = owner[...].astype(F32)
    earlier = iota((LINES, LINES), 0)
    later = iota((LINES, LINES), 1)
    diag = earlier == later

    def as_row(col):
        return jnp.sum(jnp.where(diag, col, 0.0), axis=0, keepdims=True)

    own_row = as_row(own_col)
    rank_row = jnp.sum(
        jnp.where((own_col == own_row) & (earlier < later), 1.0, 0.0), axis=0, keepdims=True
    )
    slot_row = CAP * own_row + rank_row
    chosen = iota((GROUP * CAP, LINES), 0).astype(F32) == slot_row

    def pick(row):
        return jnp.sum(jnp.where(chosen, row, 0.0), axis=1, keepdims=True)

    w = weights[...]
    q = pick(dplane[...].astype(F32))
    j = pick(dline[...].astype(F32))
    a1 = pick(as_row(w[:, 0:1]))
    a2 = pick(as_row(w[:, 1:2]))
    a3 = pick(as_row(w[:, 2:3]))
    used = pick(jnp.ones((1, LINES), F32))
    lane = iota((GROUP * CAP, NJ), 1).astype(F32)
    along_j = jnp.where(lane == j, 1.0 - a2, 0.0) + jnp.where(lane == j + 1.0, a2, 0.0)
    along_j = along_j * used
    parts = []
    for plane in range(PL):
        weight = jnp.where(q == plane, 1.0 - a1, 0.0) + jnp.where(q + 1.0 == plane, a1, 0.0)
        parts.append(weight * along_j)
    return parts, a3


def exchange_kernel(
    flow, links_in, dplane_in, dline_in, weights_in, owner_in,
    state, arrived,
    cells, links, dplane, dline, weights, owner,
    faces, chosen, got, ghost_lo, ghost_hi, sending, slots, rows, fracs,
    in_sem, s1_send, s1_recv, s2_send, s2_recv, m_send, m_recv,
):
    y = lax.axis_index("gy")
    z = lax.axis_index("gz")
    me = y * NZ + z
    a, b = z % QUAD, z // QUAD

    loads = [
        pltpu.make_async_copy(flow, cells.at[:, :, pl.ds(PAD, NJ), :], in_sem.at[0]),
        pltpu.make_async_copy(links_in, links, in_sem.at[1]),
        pltpu.make_async_copy(dplane_in, dplane, in_sem.at[2]),
        pltpu.make_async_copy(dline_in, dline, in_sem.at[3]),
        pltpu.make_async_copy(weights_in, weights, in_sem.at[4]),
        pltpu.make_async_copy(owner_in, owner, in_sem.at[5]),
    ]
    for load in loads:
        load.start()

    def peer(t):
        py = (y + t // NZ) % NY
        pz = (z + t) % NZ
        return py, pz

    barrier = pltpu.get_barrier_semaphore()

    def greet(t, carry):
        py, pz = peer(t)
        pl.semaphore_signal(barrier, inc=1, device_id={"gy": py, "gz": pz}, device_id_type=MESH)
        return carry

    lax.fori_loop(1, GROUP, greet, 0)

    for load in loads:
        load.wait()

    first_last = iota((8, NK), 0)
    lane8 = iota((8, NK), 1)
    ends = jnp.where(
        ((first_last == 0) & (lane8 == 0)) | ((first_last == 1) & (lane8 == NK - 1)), 1.0, 0.0
    )
    for v in range(VARS):
        for p in range(PL):
            layer = lax.dot_general(
                ends, cells[v, p, pl.ds(PAD, NJ), :], (((1,), (1,)), ((), ())),
                precision=EXACT, preferred_element_type=F32,
            )
            faces[0, 0, pl.ds(v * PL + p, 1), :] = layer[0:1]
            faces[0, 1, pl.ds(v * PL + p, 1), :] = layer[1:2]
    for r in range(2):
        goal = jnp.full((4, NJ), links[0, 2 * r], jnp.int32).astype(F32)
        faces[0, r, pl.ds(VARS * PL, 4), :] = goal

    pl.semaphore_wait(barrier, GROUP - 1)

    stage1 = []
    for s in range(1, QUAD):
        stage1.append(pltpu.make_async_remote_copy(
            src_ref=faces.at[0], dst_ref=faces.at[s],
            send_sem=s1_send.at[s], recv_sem=s1_recv.at[s],
            device_id={"gy": y, "gz": b * QUAD + (a + s) % QUAD}, device_id_type=MESH,
        ))
        stage1[-1].start()

    parts, a3 = slot_matrix(dplane, dline, weights, owner)
    for plane in range(PL):
        slots[:, pl.ds(plane * NJ, NJ)] = parts[plane]
    fracs[...] = jnp.broadcast_to(a3, (GROUP * CAP, NK))
    for v in range(VARS):
        lines = cells[v, :, pl.ds(PAD, NJ), :].reshape(PL * NJ, NK)
        rows[:, pl.ds(v * NK, NK)] = jnp.dot(
            slots[...], lines, precision=EXACT, preferred_element_type=F32
        )
        for p in range(PL):
            cells[v, p, pl.ds(PAD - 1, 1), :] = cells[v, p, pl.ds(PAD, 1), :]
            cells[v, p, pl.ds(PAD + NJ, 1), :] = cells[v, p, pl.ds(PAD + NJ - 1, 1), :]

    for copy in stage1:
        copy.wait()

    stage2 = []
    for s in list(range(1, QUAD)) + [0]:
        goal = (((b + s) % QUAD) * QUAD + a).astype(F32)
        for r in range(2):
            total = jnp.zeros((FACE_ROWS, NJ), F32)
            for source in range(QUAD):
                tag = faces[source, r, pl.ds(VARS * PL, 1), :]
                total = total + jnp.where(tag == goal, faces[source, r], 0.0)
            if s:
                chosen[s, r] = total
            else:
                got[0, r] = total
        if s:
            stage2.append(pltpu.make_async_remote_copy(
                src_ref=chosen.at[s], dst_ref=got.at[s],
                send_sem=s2_send.at[s], recv_sem=s2_recv.at[s],
                device_id={"gy": y, "gz": ((b + s) % QUAD) * QUAD + a}, device_id_type=MESH,
            ))
            stage2[-1].start()
    for copy in stage2:
        copy.wait()

    down = iota((NJ, NJ), 0)
    across = iota((NJ, NJ), 1)
    for r, ghost, column in ((0, ghost_hi, 3), (1, ghost_lo, 1)):
        layer = (got[0, r] + got[1, r]) + (got[2, r] + got[3, r])
        flipped = jnp.full((NJ, NJ), links[0, column], jnp.int32) == 1
        turn = jnp.where(across == jnp.where(flipped, NJ - 1 - down, down), 1.0, 0.0)
        ghost[...] = lax.dot_general(
            turn, layer, (((1,), (1,)), ((), ())), precision=EXACT, preferred_element_type=F32
        )

    lane_face = iota((GROUP * CAP, FACE_ROWS), 1)
    beyond = jnp.zeros((GROUP * CAP, FACE_ROWS), F32)
    for plane in range(PL):
        term = jnp.dot(
            slots[:, pl.ds(plane * NJ, NJ)], ghost_hi[...],
            precision=EXACT, preferred_element_type=F32,
        )
        beyond = beyond + jnp.where(lane_face % PL == plane, term, 0.0)
    lane = iota((GROUP * CAP, NK), 1)
    frac = fracs[...]
    for v in range(VARS):
        here = rows[:, pl.ds(v * NK, NK)]
        tail = jnp.sum(jnp.where(lane_face // PL == v, beyond, 0.0), axis=1, keepdims=True)
        following = jnp.where(lane == NK - 1, tail, pltpu.roll(here, NK - 1, 1))
        value = (1.0 - frac) * here + frac * following
        sending[:, :, pl.ds(v * NK, NK)] = value.reshape(GROUP, CAP, NK)

    def send(t, carry):
        py, pz = peer(t)
        pltpu.make_async_remote_copy(
            src_ref=sending.at[py * NZ + pz], dst_ref=arrived.at[me],
            send_sem=m_send, recv_sem=m_recv,
            device_id={"gy": py, "gz": pz}, device_id_type=MESH,
        ).start()
        return carry

    lax.fori_loop(1, GROUP, send, 0)
    arrived[me] = sending[me]

    lane_k = iota((8, NK), 1)

    def advance(jb, carry):
        at = pl.multiple_of(jb * 8, 8)

        def load(p, shift):
            return [cells[v, p, pl.ds(at + PAD + shift, 8), :] for v in range(VARS)]

        lo = ghost_lo[pl.ds(at, 8), :]
        hi = ghost_hi[pl.ds(at, 8), :]
        centre = [load(p, 0) for p in range(PL)]
        prim = [prims(u) for u in centre]
        across = [(centre[p],) + flux(centre[p], prim[p], 0) for p in range(PL)]
        edges = [across[0][1]]
        for p in range(PL - 1):
            edges.append(face(across[p], across[p + 1]))
        edges.append(across[PL - 1][1])
        for p in range(PL):
            u = centre[p]
            change = [edges[p + 1][v] - edges[p][v] for v in range(VARS)]
            mid = (u,) + flux(u, prim[p], 1)
            after = face(mid, side(load(p, 1), 1))
            before = face(side(load(p, -1), 1), mid)
            change = [change[v] + (after[v] - before[v]) for v in range(VARS)]
            mid = (u,) + flux(u, prim[p], 2)
            right = [
                jnp.where(lane_k == NK - 1, hi[:, v * PL + p : v * PL + p + 1], pltpu.roll(u[v], NK - 1, 1))
                for v in range(VARS)
            ]
            left = [
                jnp.where(lane_k == 0, lo[:, v * PL + p : v * PL + p + 1], pltpu.roll(u[v], 1, 1))
                for v in range(VARS)
            ]
            after = face(mid, side(right, 2))
            before = face(side(left, 2), mid)
            change = [change[v] + (after[v] - before[v]) for v in range(VARS)]
            for v in range(VARS):
                state[v, p, pl.ds(at, 8), :] = u[v] - 0.08 * change[v]
        return carry

    lax.fori_loop(0, NJ // 8, advance, 0)

    others = pl.ds(0, GROUP - 1)
    pltpu.make_async_copy(arrived.at[others], arrived.at[others], m_recv).wait()
    pltpu.make_async_copy(sending.at[others], sending.at[others], m_send).wait()


def finish_kernel(state_in, arrived, state_out, fringe, sem):
    copy = pltpu.make_async_copy(state_in, state_out, sem)
    copy.start()
    for g in range(GROUP):
        fringe[pl.ds(CAP * g, CAP), :] = arrived[g]
    copy.wait()


def local(flow_state, face_links, donor_plane, donor_line, donor_weights, receptor_owner):
    anywhere = pl.BlockSpec(memory_space=pl.ANY)
    vmem = pl.BlockSpec(memory_space=pltpu.VMEM)
    state, arrived = pl.pallas_call(
        exchange_kernel,
        out_shape=(
            jax.ShapeDtypeStruct((VARS, PL, NJ, NK), F32),
            jax.ShapeDtypeStruct((GROUP, CAP, WIDE), F32),
        ),
        in_specs=[anywhere] * 6,
        out_specs=(vmem, vmem),
        scratch_shapes=[
            pltpu.VMEM((VARS, PL, NJ + 2 * PAD, NK), F32),
            pltpu.SMEM((1, 4), jnp.int32),
            pltpu.VMEM((1, LINES), jnp.int32),
            pltpu.VMEM((1, LINES), jnp.int32),
            pltpu.VMEM((LINES, 3), F32),
            pltpu.VMEM((LINES, 1), jnp.int32),
            pltpu.VMEM((QUAD, 2, FACE_ROWS, NJ), F32),
            pltpu.VMEM((QUAD, 2, FACE_ROWS, NJ), F32),
            pltpu.VMEM((QUAD, 2, FACE_ROWS, NJ), F32),
            pltpu.VMEM((NJ, FACE_ROWS), F32),
            pltpu.VMEM((NJ, FACE_ROWS), F32),
            pltpu.VMEM((GROUP, CAP, WIDE), F32),
            pltpu.VMEM((GROUP * CAP, PL * NJ), F32),
            pltpu.VMEM((GROUP * CAP, WIDE), F32),
            pltpu.VMEM((GROUP * CAP, NK), F32),
            pltpu.SemaphoreType.DMA((6,)),
            pltpu.SemaphoreType.DMA((QUAD,)),
            pltpu.SemaphoreType.DMA((QUAD,)),
            pltpu.SemaphoreType.DMA((QUAD,)),
            pltpu.SemaphoreType.DMA((QUAD,)),
            pltpu.SemaphoreType.DMA,
            pltpu.SemaphoreType.DMA,
        ],
        compiler_params=pltpu.CompilerParams(
            collective_id=0, has_side_effects=True, vmem_limit_bytes=24 * 1024 * 1024
        ),
    )(
        flow_state.reshape(VARS, PL, NJ, NK),
        face_links.reshape(1, 4),
        donor_plane.reshape(1, LINES),
        donor_line.reshape(1, LINES),
        donor_weights.reshape(LINES, 3),
        receptor_owner.reshape(LINES, 1),
    )
    new_state, fringe = pl.pallas_call(
        finish_kernel,
        out_shape=(
            jax.ShapeDtypeStruct((VARS, PL, NJ, NK), F32),
            jax.ShapeDtypeStruct((GROUP * CAP, WIDE), F32),
        ),
        in_specs=[anywhere, vmem],
        out_specs=(anywhere, vmem),
        scratch_shapes=[pltpu.SemaphoreType.DMA],
        compiler_params=pltpu.CompilerParams(vmem_limit_bytes=16 * 1024 * 1024),
    )(state, arrived)
    return (
        new_state.reshape(1, 1, 1, VARS, PL, NJ, NK),
        fringe.reshape(1, 1, 1, GROUP * CAP, WIDE),
    )


def solution(mesh):
    return jax.shard_map(
        local,
        mesh=mesh,
        in_specs=(
            P("gx", "gy", "gz", None, None, None, None),
            P("gx", "gy", "gz", None),
            P("gx", "gy", "gz", None),
            P("gx", "gy", "gz", None),
            P("gx", "gy", "gz", None, None),
            P("gx", "gy", "gz", None, None),
        ),
        out_specs=(P("gx", "gy", "gz", None, None, None, None), P("gx", "gy", "gz", None, None)),
        check_vma=False,
    )
```

time: 120 us -> 55.4 us (0.46)
  the two profiles are of different devices: /device:TPU:2 before, /device:TPU:4 now
where the time goes in v1:
time: 55.4 us; the launch traced here: 55.2 us
  Pallas kernels  49.8 us (90%)
  local copies, waits for them, and re-layouts  4.79 us (9%)
  between operations  0.64 us (1%)
    pallas_call x1, Pallas kernels, local(): pl.pallas_call(exchange_kernel, out_shape=(jax.ShapeDtypeStruct((VARS, PL...  48 us
    unnamed x9, local copies, waits for them, and re-layouts  4.05 us
    pallas_call x1, Pallas kernels, local(): pl.pallas_call(finish_kernel, out_shape=(jax.ShapeDtypeStruct((VARS, PL,...  1.79 us

profile of v1, /device:TPU:4, one launch (start us, length us, event | category | flops | bytes accessed | tf_op | source)
XLA Modules:
  0.0 55.2 jit_solution(369674926914202549)
XLA Ops:
  0.6 0.8 %copy.8 = f32[1,1,1,64,3]{4,3,2,1,0:T(8,128)S(1)} copy(f32[1,1,1,64,3]{3,2,4,1,0:T(1,128)} %param.10) | data formatting | bytes 1536 | tf_op args[4]
  1.4 0.7 %copy.9.owner_in = s32[64,1]{1,0:T(8,128)S(1)} copy(s32[64,1]{0,1:T(1,128)} %bitcast.13) | data formatting | bytes 512 | tf_op jit(solution)/shard_map/reshape | solution.py:334
  2.1 0.0 copy-start
  2.1 1.3 %copy-done = f32[1,1,1,5,4,128,128]{6,5,4,3,2,1,0:T(8,128)S(1)} copy-done((f32[1,1,1,5,4,128,128]{6,5,4,3,2,1,0:T(8,128)S(1)}, f32[1,1,1,5,4,128,128]{6,5,4,3,2,1,0:T(8,128)}, u32[]{:S(2)}) %copy-start) | copy-done | bytes 1310744
  3.5 0.0 copy-start.1
  3.5 0.7 %copy-done.1 = s32[1,1,1,4]{3,2,1,0:T(1,128)S(1)} copy-done((s32[1,1,1,4]{3,2,1,0:T(1,128)S(1)}, s32[1,1,1,4]{3,2,1,0:T(1,128)}, u32[]{:S(2)}) %copy-start.1) | copy-done | bytes 40
  4.1 0.0 copy-start.2
  4.1 0.7 %copy-done.2 = s32[1,1,1,64]{3,2,1,0:T(1,128)S(1)} copy-done((s32[1,1,1,64]{3,2,1,0:T(1,128)S(1)}, s32[1,1,1,64]{3,2,1,0:T(1,128)}, u32[]{:S(2)}) %copy-start.2) | copy-done | bytes 280
  4.8 0.0 copy-start.3
  4.8 0.7 %copy-done.3 = s32[1,1,1,64]{3,2,1,0:T(1,128)S(1)} copy-done((s32[1,1,1,64]{3,2,1,0:T(1,128)S(1)}, s32[1,1,1,64]{3,2,1,0:T(1,128)}, u32[]{:S(2)}) %copy-start.3) | copy-done | bytes 280
  5.4 48.0 %shard_map.77 = (f32[5,4,128,128]{3,2,1,0:T(8,128)S(1)}, f32[64,2,640]{2,1,0:T(2,128)S(1)}) custom-call(f32[5,4,128,128]{3,2,1,0:T(8,128)S(1)} %bitcast.8, s32[1,4]{1,0:T(1,128)S(1)} %bitcast.10, s32[1,64]{1,0:T(1,128)S(1)} %bitcast.11, s32[1,64]{1,0:T(1,128)S(1)} %bitcast.12, f32[64,3]{1,0:T(8,128)S(1)} %bitcast.9, s32[64,1]{1,0:T(8,128)S(1)} %copy.9.owner_in), custom_call_target="tpu_custom_call" | custom-call | tf_op jit(solution)/shard_map/pallas_call | solution.py:293
  53.4 1.8 %shard_map.78 = (f32[5,4,128,128]{3,2,1,0:T(8,128)}, f32[128,640]{1,0:T(8,128)}) custom-call(f32[5,4,128,128]{3,2,1,0:T(8,128)S(1)} %get-tuple-element.6.state_in, f32[64,2,640]{2,1,0:T(2,128)S(1)} %get-tuple-element.7.arrived), custom_call_target="tpu_custom_call" | custom-call | tf_op jit(solution)/shard_map/pallas_call | solution.py:336
Async XLA Ops:
  2.1 1.3 %copy-start = (f32[1,1,1,5,4,128,128]{6,5,4,3,2,1,0:T(8,128)S(1)}, f32[1,1,1,5,4,128,128]{6,5,4,3,2,1,0:T(8,128)}, u32[]{:S(2)}) copy-start(f32[1,1,1,5,4,128,128]{6,5,4,3,2,1,0:T(8,128)} %param.6) | copy-start | bytes 3932164
  3.5 0.7 %copy-start.1 = (s32[1,1,1,4]{3,2,1,0:T(1,128)S(1)}, s32[1,1,1,4]{3,2,1,0:T(1,128)}, u32[]{:S(2)}) copy-start(s32[1,1,1,4]{3,2,1,0:T(1,128)} %param.7) | copy-start | bytes 52
  4.1 0.7 %copy-start.2 = (s32[1,1,1,64]{3,2,1,0:T(1,128)S(1)}, s32[1,1,1,64]{3,2,1,0:T(1,128)}, u32[]{:S(2)}) copy-start(s32[1,1,1,64]{3,2,1,0:T(1,128)} %param.8) | copy-start | bytes 772
  4.8 0.7 %copy-start.3 = (s32[1,1,1,64]{3,2,1,0:T(1,128)S(1)}, s32[1,1,1,64]{3,2,1,0:T(1,128)}, u32[]{:S(2)}) copy-start(s32[1,1,1,64]{3,2,1,0:T(1,128)} %param.9) | copy-start | bytes 772

commit v2 on v1

v2 whole, which is shorter than its diff:
```python
import jax
import jax.numpy as jnp
from jax import lax
from jax.experimental import pallas as pl
from jax.experimental.pallas import tpu as pltpu
from jax.sharding import PartitionSpec as P

MESH = pl.DeviceIdType.MESH
EXACT = lax.Precision.HIGHEST
NY, NZ, QUAD = 4, 16, 4
HALF = NZ // 2
GROUP, CAP = 64, 2
EARLY = 16
VARS, PL, NJ, NK = 5, 4, 128, 128
LINES = 64
PAD = 8
WIDE = VARS * NK
FACE_ROWS = 24
F32 = jnp.float32
ROOM = 60 * 1024 * 1024


def iota(shape, dim):
    return lax.broadcasted_iota(jnp.int32, shape, dim)


def prims(u):
    r = 1.0 / u[0]
    vel = [u[1] * r, u[2] * r, u[3] * r]
    kinetic = u[1] * vel[0] + u[2] * vel[1] + u[3] * vel[2]
    p = 0.4 * (u[4] - 0.5 * kinetic)
    return vel, p, jnp.sqrt(1.4 * p * r)


def flux(u, prim, d):
    vel, p, cs = prim
    n = vel[d]
    f = [u[1 + d]]
    for c in range(3):
        t = u[1 + c] * n
        f.append(t + p if c == d else t)
    f.append((u[4] + p) * n)
    return f, jnp.abs(n) + cs


def face(left, right):
    (ul, fl, sl), (ur, fr, sr) = left, right
    a = jnp.maximum(sl, sr)
    return [0.5 * (fl[v] + fr[v]) - 0.5 * a * (ur[v] - ul[v]) for v in range(VARS)]


def side(u, d):
    f, s = flux(u, prims(u), d)
    return u, f, s


def line_fields(dplane, dline, weights, owner):
    own_row = owner[...].astype(F32)
    earlier = iota((LINES, LINES), 0)
    later = iota((LINES, LINES), 1)
    own_col = jnp.sum(jnp.where(earlier == later, own_row, 0.0), axis=1, keepdims=True)
    rank_row = jnp.sum(
        jnp.where((own_col == own_row) & (earlier < later), 1.0, 0.0), axis=0, keepdims=True
    )
    slot_row = CAP * own_row + rank_row
    return [
        slot_row, dplane[...].astype(F32), dline[...].astype(F32), weights[0], weights[1], weights[2]
    ]


def slot_matrix(fields, lane):
    slot_row = fields[0]
    chosen = iota((GROUP * CAP, LINES), 0).astype(F32) == slot_row

    def pick(row):
        return jnp.sum(jnp.where(chosen, row, 0.0), axis=1, keepdims=True)

    q, j, a1, a2, a3 = [pick(row) for row in fields[1:]]
    used = pick(jnp.ones((1, LINES), F32))
    along_j = jnp.where(lane == j, 1.0 - a2, 0.0) + jnp.where(lane == j + 1.0, a2, 0.0)
    along_j = along_j * used
    parts = []
    for plane in range(PL):
        weight = jnp.where(q == plane, 1.0 - a1, 0.0) + jnp.where(q + 1.0 == plane, a1, 0.0)
        parts.append(weight * along_j)
    return parts, a3


def exchange_kernel(
    flow, links_in, dplane_in, dline_in, weights_in, owner_in,
    state_out, fringe_out,
    state, arrived, fringe, cells, links, dplane, dline, weights, owner,
    faces, chosen, got, ghost_lo, ghost_hi, sending, slots, rows, fracs, ends_out, ends_in, notes,
    in_sem, s1_send, s1_recv, s2_send, s2_recv, m_send, m_recv, e_send, e_recv, n_send, n_recv, out_sem,
):
    y = lax.axis_index("gy")
    z = lax.axis_index("gz")
    me = y * NZ + z
    a, b = z % QUAD, z // QUAD

    loads = [
        pltpu.make_async_copy(flow, cells.at[:, :, pl.ds(PAD, NJ), :], in_sem.at[0]),
        pltpu.make_async_copy(links_in, links, in_sem.at[1]),
        pltpu.make_async_copy(dplane_in, dplane, in_sem.at[2]),
        pltpu.make_async_copy(dline_in, dline, in_sem.at[3]),
        pltpu.make_async_copy(weights_in, weights, in_sem.at[4]),
        pltpu.make_async_copy(owner_in, owner, in_sem.at[5]),
    ]
    for load in loads:
        load.start()

    def peer(i):
        d = HALF - (i + 4) // 8
        dz = jnp.where(i % 2 == 0, d, NZ - d)
        dy = jnp.where(d == HALF, i, jnp.where(d == 0, i - 59, (i - 4) // 2))
        return (y + dy) % NY, (z + jnp.where(d == HALF, HALF, dz)) % NZ

    barrier = pltpu.get_barrier_semaphore()

    def greet(i, carry):
        py, pz = peer(i)
        pl.semaphore_signal(barrier, inc=1, device_id={"gy": py, "gz": pz}, device_id_type=MESH)
        return carry

    lax.fori_loop(0, GROUP - 1, greet, 0)

    for load in loads:
        load.wait()

    first_last = iota((8, NK), 0)
    lane8 = iota((8, NK), 1)
    ends = jnp.where(
        ((first_last == 0) & (lane8 == 0)) | ((first_last == 1) & (lane8 == NK - 1)), 1.0, 0.0
    )
    for v in range(VARS):
        for p in range(PL):
            layer = lax.dot_general(
                ends, cells[v, p, pl.ds(PAD, NJ), :], (((1,), (1,)), ((), ())),
                precision=EXACT, preferred_element_type=F32,
            )
            faces[0, 0, pl.ds(v * PL + p, 1), :] = layer[0:1]
            faces[0, 1, pl.ds(v * PL + p, 1), :] = layer[1:2]
    for r in range(2):
        goal = jnp.full((4, NJ), links[0, 2 * r], jnp.int32).astype(F32)
        faces[0, r, pl.ds(VARS * PL, 4), :] = goal

    lane = iota((GROUP * CAP, NK), 1)
    fields = line_fields(dplane, dline, weights, owner)
    lane_f = lane.astype(F32)
    parts, a3 = slot_matrix(fields, lane_f)
    for plane in range(PL):
        slots[:, pl.ds(plane * NJ, NJ)] = parts[plane]
    fracs[...] = jnp.broadcast_to(a3, (GROUP * CAP, NK))
    for v in range(VARS):
        lines = cells[v, :, pl.ds(PAD, NJ), :].reshape(PL * NJ, NK)
        rows[:, pl.ds(v * NK, NK)] = jnp.dot(
            slots[...], lines, precision=EXACT, preferred_element_type=F32
        )
        for p in range(PL):
            cells[v, p, pl.ds(PAD - 1, 1), :] = cells[v, p, pl.ds(PAD, 1), :]
            cells[v, p, pl.ds(PAD + NJ, 1), :] = cells[v, p, pl.ds(PAD + NJ - 1, 1), :]

    target = jnp.full((1, LINES), links[0, 2], jnp.int32).astype(F32)
    held = fields + [target, target]
    for row in range(4):
        notes[z, pl.ds(row, 1), :] = jnp.concatenate(held[2 * row : 2 * row + 2], axis=1)

    frac = fracs[...]
    for v in range(VARS):
        here = rows[:, pl.ds(v * NK, NK)]
        following = jnp.where(lane == NK - 1, 0.0, pltpu.roll(here, NK - 1, 1))
        value = (1.0 - frac) * here + frac * following
        sending[:, :, pl.ds(v * NK, NK)] = value.reshape(GROUP, CAP, NK)

    pl.semaphore_wait(barrier, GROUP - 1)

    def send_notes(d, carry):
        pltpu.make_async_remote_copy(
            src_ref=notes.at[z], dst_ref=notes.at[z], send_sem=n_send, recv_sem=n_recv,
            device_id={"gy": y, "gz": (z + jnp.where(d % 2 == 1, NZ - d // 2, d // 2)) % NZ},
            device_id_type=MESH,
        ).start()
        return carry

    lax.fori_loop(0, NZ - 1, lambda i, c: send_notes(NZ - i, c), 0)
    stage1 = []
    for s in range(1, QUAD):
        stage1.append(pltpu.make_async_remote_copy(
            src_ref=faces.at[0], dst_ref=faces.at[s],
            send_sem=s1_send.at[s], recv_sem=s1_recv.at[s],
            device_id={"gy": y, "gz": b * QUAD + (a + s) % QUAD}, device_id_type=MESH,
        ))
        stage1[-1].start()

    def send(i, carry):
        py, pz = peer(i)
        pltpu.make_async_remote_copy(
            src_ref=sending.at[py * NZ + pz], dst_ref=arrived.at[me],
            send_sem=m_send, recv_sem=m_recv,
            device_id={"gy": py, "gz": pz}, device_id_type=MESH,
        ).start()
        return carry

    lax.fori_loop(0, EARLY, send, 0)
    lane_k = iota((8, NK), 1)

    def load(at, p, shift):
        return [cells[v, p, pl.ds(at + PAD + shift, 8), :] for v in range(VARS)]

    def advance(jb, carry):
        at = pl.multiple_of(jb * 8, 8)
        centre = [load(at, p, 0) for p in range(PL)]
        prim = [prims(u) for u in centre]
        layers = [(centre[p],) + flux(centre[p], prim[p], 0) for p in range(PL)]
        edges = [layers[0][1]]
        for p in range(PL - 1):
            edges.append(face(layers[p], layers[p + 1]))
        edges.append(layers[PL - 1][1])
        for p in range(PL):
            u = centre[p]
            mid = (u,) + flux(u, prim[p], 1)
            after = face(mid, side(load(at, p, 1), 1))
            before = face(side(load(at, p, -1), 1), mid)
            for v in range(VARS):
                change = (edges[p + 1][v] - edges[p][v]) + (after[v] - before[v])
                state[v, p, pl.ds(at, 8), :] = u[v] - 0.08 * change
        return carry

    lax.fori_loop(0, NJ // 8, advance, 0)

    for copy in stage1:
        copy.wait()

    stage2 = []
    for s in list(range(1, QUAD)) + [0]:
        goal = (((b + s) % QUAD) * QUAD + a).astype(F32)
        for r in range(2):
            total = jnp.zeros((FACE_ROWS, NJ), F32)
            for source in range(QUAD):
                tag = faces[source, r, pl.ds(VARS * PL, 1), :]
                total = total + jnp.where(tag == goal, faces[source, r], 0.0)
            if s:
                chosen[s, r] = total
            else:
                got[0, r] = total
        if s:
            stage2.append(pltpu.make_async_remote_copy(
                src_ref=chosen.at[s], dst_ref=got.at[s],
                send_sem=s2_send.at[s], recv_sem=s2_recv.at[s],
                device_id={"gy": y, "gz": ((b + s) % QUAD) * QUAD + a}, device_id_type=MESH,
            ))
            stage2[-1].start()
    in_line = pl.ds(0, NZ - 1)
    pltpu.make_async_copy(notes.at[in_line], notes.at[in_line], n_recv).wait()
    wanted = jnp.zeros((4, 2 * LINES), F32)
    for source in range(NZ):
        note = notes[source]
        wanted = wanted + jnp.where(note[3:4, 0:1] == z.astype(F32), note, 0.0)
    theirs = []
    for row in range(3):
        theirs += [wanted[row : row + 1, 0:LINES], wanted[row : row + 1, LINES:]]
    flipped = jnp.full((GROUP * CAP, NJ), links[0, 1], jnp.int32) == 1
    parts, a3 = slot_matrix(theirs, jnp.where(flipped, NJ - 1.0 - lane_f, lane_f))
    lane_face = iota((GROUP * CAP, FACE_ROWS), 1)
    beyond = jnp.zeros((GROUP * CAP, FACE_ROWS), F32)
    for plane in range(PL):
        term = lax.dot_general(
            parts[plane], faces[0, 0], (((1,), (1,)), ((), ())),
            precision=EXACT, preferred_element_type=F32,
        )
        beyond = beyond + jnp.where(lane_face % PL == plane, term, 0.0)
    last = jnp.where(lane == VARS, jnp.full((GROUP * CAP, NK), links[0, 0], jnp.int32).astype(F32), 0.0)
    for v in range(VARS):
        tail = jnp.sum(jnp.where(lane_face // PL == v, beyond, 0.0), axis=1, keepdims=True)
        last = last + jnp.where(lane == v, a3 * tail, 0.0)
    ends_out[...] = last.reshape(GROUP, CAP, NK)

    def send_ends(i, carry):
        py, pz = peer(i)
        pltpu.make_async_remote_copy(
            src_ref=ends_out.at[py * NZ + pz], dst_ref=ends_in.at[me],
            send_sem=e_send, recv_sem=e_recv,
            device_id={"gy": py, "gz": pz}, device_id_type=MESH,
        ).start()
        return carry

    lax.fori_loop(0, GROUP - 1, send_ends, 0)
    ends_in[me] = ends_out[me]

    lax.fori_loop(EARLY, GROUP - 1, send, 0)
    arrived[me] = sending[me]

    for copy in stage2:
        copy.wait()

    down = iota((NJ, NJ), 0)
    across = iota((NJ, NJ), 1)
    for r, ghost, column in ((0, ghost_hi, 3), (1, ghost_lo, 1)):
        layer = (got[0, r] + got[1, r]) + (got[2, r] + got[3, r])
        flipped = jnp.full((NJ, NJ), links[0, column], jnp.int32) == 1
        turn = jnp.where(across == jnp.where(flipped, NJ - 1 - down, down), 1.0, 0.0)
        ghost[...] = lax.dot_general(
            turn, layer, (((1,), (1,)), ((), ())), precision=EXACT, preferred_element_type=F32
        )

    def advance_k(jb, carry):
        at = pl.multiple_of(jb * 8, 8)
        lo = ghost_lo[pl.ds(at, 8), :]
        hi = ghost_hi[pl.ds(at, 8), :]
        for p in range(PL):
            u = load(at, p, 0)
            mid = side(u, 2)
            right = [
                jnp.where(lane_k == NK - 1, hi[:, v * PL + p : v * PL + p + 1], pltpu.roll(u[v], NK - 1, 1))
                for v in range(VARS)
            ]
            left = [
                jnp.where(lane_k == 0, lo[:, v * PL + p : v * PL + p + 1], pltpu.roll(u[v], 1, 1))
                for v in range(VARS)
            ]
            after = face(mid, side(right, 2))
            before = face(side(left, 2), mid)
            for v in range(VARS):
                old = state[v, p, pl.ds(at, 8), :]
                state[v, p, pl.ds(at, 8), :] = old - 0.08 * (after[v] - before[v])
        return carry

    lax.fori_loop(0, NJ // 8, advance_k, 0)
    put_state = pltpu.make_async_copy(state, state_out, out_sem.at[0])
    put_state.start()

    others = pl.ds(0, GROUP - 1)
    pltpu.make_async_copy(ends_in.at[others], ends_in.at[others], e_recv).wait()
    for g in range(GROUP):
        rows[pl.ds(CAP * g, CAP), pl.ds(0, NK)] = ends_in[g]
    came = rows[:, pl.ds(0, NK)]
    slot = iota((GROUP * CAP, GROUP * CAP), 0)
    place = iota((GROUP * CAP, GROUP * CAP), 1)
    donor_z = jnp.sum(jnp.where(slot == place, came[:, VARS : VARS + 1], 0.0), axis=0, keepdims=True)
    home = place // (CAP * NZ) * (CAP * NZ) + place % CAP
    move = jnp.where(slot.astype(F32) == home.astype(F32) + CAP * donor_z, 1.0, 0.0)
    gained = jnp.dot(move, came, precision=EXACT, preferred_element_type=F32)

    pltpu.make_async_copy(arrived.at[others], arrived.at[others], m_recv).wait()
    for g in range(GROUP):
        fringe[pl.ds(CAP * g, CAP), :] = arrived[g]
    for v in range(VARS):
        here = fringe[:, pl.ds(v * NK, NK)]
        fringe[:, pl.ds(v * NK, NK)] = here + jnp.where(lane == NK - 1, gained[:, v : v + 1], 0.0)
    put_fringe = pltpu.make_async_copy(fringe, fringe_out, out_sem.at[1])
    put_fringe.start()
    pltpu.make_async_copy(sending.at[others], sending.at[others], m_send).wait()
    pltpu.make_async_copy(ends_out.at[others], ends_out.at[others], e_send).wait()
    pltpu.make_async_copy(notes.at[in_line], notes.at[in_line], n_send).wait()
    put_state.wait()
    put_fringe.wait()


def finish_kernel(state_in, fringe_in, state_out, fringe_out, state, fringe, in_sem, out_sem):
    trips = [(fringe_in, fringe, fringe_out)]
    for v in range(VARS):
        trips.append((state_in.at[v], state.at[v], state_out.at[v]))
    inward = [pltpu.make_async_copy(t[0], t[1], in_sem.at[i]) for i, t in enumerate(trips)]
    outward = [pltpu.make_async_copy(t[1], t[2], out_sem.at[i]) for i, t in enumerate(trips)]
    for copy in inward:
        copy.start()
    for first, second in zip(inward, outward):
        first.wait()
        second.start()
    for copy in outward:
        copy.wait()


def local(flow_state, face_links, donor_plane, donor_line, donor_weights, receptor_owner):
    anywhere = pl.BlockSpec(memory_space=pl.ANY)
    state, arrived = pl.pallas_call(
        exchange_kernel,
        out_shape=(
            jax.ShapeDtypeStruct((VARS, PL, NJ, NK), F32),
            jax.ShapeDtypeStruct((GROUP * CAP, WIDE), F32),
        ),
        in_specs=[anywhere] * 6,
        out_specs=(anywhere, anywhere),
        scratch_shapes=[
            pltpu.VMEM((VARS, PL, NJ, NK), F32),
            pltpu.VMEM((GROUP, CAP, WIDE), F32),
            pltpu.VMEM((GROUP * CAP, WIDE), F32),
            pltpu.VMEM((VARS, PL, NJ + 2 * PAD, NK), F32),
            pltpu.SMEM((1, 4), jnp.int32),
            pltpu.VMEM((1, LINES), jnp.int32),
            pltpu.VMEM((1, LINES), jnp.int32),
            pltpu.VMEM((3, 1, LINES), F32),
            pltpu.VMEM((1, LINES), jnp.int32),
            pltpu.VMEM((QUAD, 2, FACE_ROWS, NJ), F32),
            pltpu.VMEM((QUAD, 2, FACE_ROWS, NJ), F32),
            pltpu.VMEM((QUAD, 2, FACE_ROWS, NJ), F32),
            pltpu.VMEM((NJ, FACE_ROWS), F32),
            pltpu.VMEM((NJ, FACE_ROWS), F32),
            pltpu.VMEM((GROUP, CAP, WIDE), F32),
            pltpu.VMEM((GROUP * CAP, PL * NJ), F32),
            pltpu.VMEM((GROUP * CAP, WIDE), F32),
            pltpu.VMEM((GROUP * CAP, NK), F32),
            pltpu.VMEM((GROUP, CAP, NK), F32),
            pltpu.VMEM((GROUP, CAP, NK), F32),
            pltpu.VMEM((NZ, 4, 2 * LINES), F32),
            pltpu.SemaphoreType.DMA((6,)),
            pltpu.SemaphoreType.DMA((QUAD,)),
            pltpu.SemaphoreType.DMA((QUAD,)),
            pltpu.SemaphoreType.DMA((QUAD,)),
            pltpu.SemaphoreType.DMA((QUAD,)),
            pltpu.SemaphoreType.DMA,
            pltpu.SemaphoreType.DMA,
            pltpu.SemaphoreType.DMA,
            pltpu.SemaphoreType.DMA,
            pltpu.SemaphoreType.DMA,
            pltpu.SemaphoreType.DMA,
            pltpu.SemaphoreType.DMA((2,)),
        ],
        compiler_params=pltpu.CompilerParams(
            collective_id=0, has_side_effects=True, vmem_limit_bytes=ROOM
        ),
    )(
        flow_state.reshape(VARS, PL, NJ, NK),
        face_links.reshape(1, 4),
        donor_plane.reshape(1, LINES),
        donor_line.reshape(1, LINES),
        jnp.transpose(donor_weights, (0, 1, 4, 2, 3)).reshape(3, 1, LINES),
        receptor_owner.reshape(1, LINES),
    )
    new_state, fringe = pl.pallas_call(
        finish_kernel,
        out_shape=(
            jax.ShapeDtypeStruct((VARS, PL, NJ, NK), F32),
            jax.ShapeDtypeStruct((GROUP * CAP, WIDE), F32),
        ),
        in_specs=[anywhere, anywhere],
        out_specs=(anywhere, anywhere),
        scratch_shapes=[
            pltpu.VMEM((VARS, PL, NJ, NK), F32),
            pltpu.VMEM((GROUP * CAP, WIDE), F32),
            pltpu.SemaphoreType.DMA((1 + VARS,)),
            pltpu.SemaphoreType.DMA((1 + VARS,)),
        ],
        compiler_params=pltpu.CompilerParams(vmem_limit_bytes=ROOM),
    )(state, arrived)
    return (
        new_state.reshape(1, 1, 1, VARS, PL, NJ, NK),
        fringe.reshape(1, 1, 1, GROUP * CAP, WIDE),
    )


def solution(mesh):
    return jax.shard_map(
        local,
        mesh=mesh,
        in_specs=(
            P("gx", "gy", "gz", None, None, None, None),
            P("gx", "gy", "gz", None),
            P("gx", "gy", "gz", None),
            P("gx", "gy", "gz", None),
            P("gx", "gy", "gz", None, None),
            P("gx", "gy", "gz", None, None),
        ),
        out_specs=(P("gx", "gy", "gz", None, None, None, None), P("gx", "gy", "gz", None, None)),
        check_vma=False,
    )
```

time: 55.4 us -> 48.4 us (0.87)
  the two profiles are of different devices: /device:TPU:4 before, /device:TPU:1 now
where the time goes in v2:
time: 48.4 us; the launch traced here: 47.9 us
  Pallas kernels  47.3 us (98%)
  between operations  0.64 us (1%)
    pallas_call x1, Pallas kernels, local(): pl.pallas_call(exchange_kernel, out_shape=(jax.ShapeDtypeStruct((VARS, PL...  45 us
    pallas_call x1, Pallas kernels, local(): pl.pallas_call(finish_kernel, out_shape=(jax.ShapeDtypeStruct((VARS, PL,...  2.23 us

profile of v2, /device:TPU:1, one launch (start us, length us, event | category | flops | bytes accessed | tf_op | source)
XLA Modules:
  0.0 47.9 jit_solution(14575429843557519462)
XLA Ops:
  0.6 45.0 %shard_map.77 = (f32[5,4,128,128]{3,2,1,0:T(8,128)}, f32[128,640]{1,0:T(8,128)}) custom-call(f32[5,4,128,128]{3,2,1,0:T(8,128)} %bitcast.10, s32[1,4]{1,0:T(1,128)} %bitcast.12, s32[1,64]{1,0:T(1,128)} %bitcast.13, s32[1,64]{1,0:T(1,128)} %bitcast.14, f32[3,1,64]{2,1,0:T(1,128)} %bitcast.11, s32[1,64]{1,0:T(1,128)} %bitcast.15), custom_call_target="tpu_custom_call" | custom-call | tf_op jit(solution)/shard_map/pallas_call | solution.py:376
  45.7 2.2 %shard_map.78 = (f32[5,4,128,128]{3,2,1,0:T(8,128)}, f32[128,640]{1,0:T(8,128)}) custom-call(f32[5,4,128,128]{3,2,1,0:T(8,128)} %get-tuple-element.6.state_in, f32[128,640]{1,0:T(8,128)} %get-tuple-element.7.fringe_in), custom_call_target="tpu_custom_call" | custom-call | tf_op jit(solution)/shard_map/pallas_call | solution.py:430

commit v3 on v2

--- a/solution.py
+++ b/solution.py
@@ -10,12 +10,13 @@
 NY, NZ, QUAD = 4, 16, 4
 HALF = NZ // 2
 GROUP, CAP = 64, 2
-EARLY = 16
+EARLY = 8
+TAG = 40
 VARS, PL, NJ, NK = 5, 4, 128, 128
 LINES = 64
 PAD = 8
 WIDE = VARS * NK
-FACE_ROWS = 24
+LAYER = VARS * PL
 F32 = jnp.float32
 ROOM = 60 * 1024 * 1024
 
@@ -90,8 +91,8 @@
     flow, links_in, dplane_in, dline_in, weights_in, owner_in,
     state_out, fringe_out,
     state, arrived, fringe, cells, links, dplane, dline, weights, owner,
-    faces, chosen, got, ghost_lo, ghost_hi, sending, slots, rows, fracs, ends_out, ends_in, notes,
-    in_sem, s1_send, s1_recv, s2_send, s2_recv, m_send, m_recv, e_send, e_recv, n_send, n_recv, out_sem,
+    faces, chosen, got, ghost_lo, ghost_hi, sending, slots, rows, fracs, ends_out, ends_in, notes, tags,
+    in_sem, s1_send, s1_recv, s2_send, s2_recv, m_send, m_recv, e_send, e_recv, n_send, n_recv, t_send, t_recv, f_send, f_recv, out_sem,
 ):
     y = lax.axis_index("gy")
     z = lax.axis_index("gz")
@@ -138,11 +139,10 @@
                 ends, cells[v, p, pl.ds(PAD, NJ), :], (((1,), (1,)), ((), ())),
                 precision=EXACT, preferred_element_type=F32,
             )
-            faces[0, 0, pl.ds(v * PL + p, 1), :] = layer[0:1]
-            faces[0, 1, pl.ds(v * PL + p, 1), :] = layer[1:2]
+            faces[0, pl.ds(v * PL + p, 1), :] = layer[0:1]
+            faces[0, pl.ds(LAYER + v * PL + p, 1), :] = layer[1:2]
     for r in range(2):
-        goal = jnp.full((4, NJ), links[0, 2 * r], jnp.int32).astype(F32)
-        faces[0, r, pl.ds(VARS * PL, 4), :] = goal
+        tags[0, pl.ds(r, 1), :] = jnp.full((1, NJ), links[0, 2 * r], jnp.int32).astype(F32)
 
     lane = iota((GROUP * CAP, NK), 1)
     fields = line_fields(dplane, dline, weights, owner)
@@ -160,10 +160,8 @@
             cells[v, p, pl.ds(PAD - 1, 1), :] = cells[v, p, pl.ds(PAD, 1), :]
             cells[v, p, pl.ds(PAD + NJ, 1), :] = cells[v, p, pl.ds(PAD + NJ - 1, 1), :]
 
-    target = jnp.full((1, LINES), links[0, 2], jnp.int32).astype(F32)
-    held = fields + [target, target]
-    for row in range(4):
-        notes[z, pl.ds(row, 1), :] = jnp.concatenate(held[2 * row : 2 * row + 2], axis=1)
+    for row in range(3):
+        notes[z, row] = jnp.concatenate(fields[2 * row : 2 * row + 2], axis=1)
 
     frac = fracs[...]
     for v in range(VARS):
@@ -185,12 +183,13 @@
     lax.fori_loop(0, NZ - 1, lambda i, c: send_notes(NZ - i, c), 0)
     stage1 = []
     for s in range(1, QUAD):
-        stage1.append(pltpu.make_async_remote_copy(
-            src_ref=faces.at[0], dst_ref=faces.at[s],
-            send_sem=s1_send.at[s], recv_sem=s1_recv.at[s],
-            device_id={"gy": y, "gz": b * QUAD + (a + s) % QUAD}, device_id_type=MESH,
-        ))
-        stage1[-1].start()
+        for buffer, send_sem, recv_sem in ((faces, s1_send, s1_recv), (tags, t_send, t_recv)):
+            stage1.append(pltpu.make_async_remote_copy(
+                src_ref=buffer.at[0], dst_ref=buffer.at[s],
+                send_sem=send_sem.at[s], recv_sem=recv_sem.at[s],
+                device_id={"gy": y, "gz": b * QUAD + (a + s) % QUAD}, device_id_type=MESH,
+            ))
+            stage1[-1].start()
 
     def send(i, carry):
         py, pz = peer(i)
@@ -232,17 +231,17 @@
         copy.wait()
 
     stage2 = []
+    is_first = iota((2 * LAYER, NJ), 0) < LAYER
     for s in list(range(1, QUAD)) + [0]:
         goal = (((b + s) % QUAD) * QUAD + a).astype(F32)
-        for r in range(2):
-            total = jnp.zeros((FACE_ROWS, NJ), F32)
-            for source in range(QUAD):
-                tag = faces[source, r, pl.ds(VARS * PL, 1), :]
-                total = total + jnp.where(tag == goal, faces[source, r], 0.0)
-            if s:
-                chosen[s, r] = total
-            else:
-                got[0, r] = total
+        total = jnp.zeros((2 * LAYER, NJ), F32)
+        for source in range(QUAD):
+            tag = jnp.where(is_first, tags[source, pl.ds(0, 1), :], tags[source, pl.ds(1, 1), :])
+            total = total + jnp.where(tag == goal, faces[source], 0.0)
+        if s:
+            chosen[s] = total
+        else:
+            got[0] = total
         if s:
             stage2.append(pltpu.make_async_remote_copy(
                 src_ref=chosen.at[s], dst_ref=got.at[s],
@@ -252,51 +251,69 @@
             stage2[-1].start()
     in_line = pl.ds(0, NZ - 1)
     pltpu.make_async_copy(notes.at[in_line], notes.at[in_line], n_recv).wait()
-    wanted = jnp.zeros((4, 2 * LINES), F32)
-    for source in range(NZ):
-        note = notes[source]
-        wanted = wanted + jnp.where(note[3:4, 0:1] == z.astype(F32), note, 0.0)
+    below = jnp.full((1, 2 * LINES), links[0, 0], jnp.int32)
     theirs = []
     for row in range(3):
-        theirs += [wanted[row : row + 1, 0:LINES], wanted[row : row + 1, LINES:]]
+        wanted = jnp.zeros((1, 2 * LINES), F32)
+        for source in range(NZ):
+            wanted = wanted + jnp.where(below == source, notes[source, row], 0.0)
+        theirs += [wanted[:, 0:LINES], wanted[:, LINES:]]
     flipped = jnp.full((GROUP * CAP, NJ), links[0, 1], jnp.int32) == 1
     parts, a3 = slot_matrix(theirs, jnp.where(flipped, NJ - 1.0 - lane_f, lane_f))
-    lane_face = iota((GROUP * CAP, FACE_ROWS), 1)
-    beyond = jnp.zeros((GROUP * CAP, FACE_ROWS), F32)
+    lane_face = iota((GROUP * CAP, 2 * LAYER), 1)
+    beyond = jnp.zeros((GROUP * CAP, 2 * LAYER), F32)
     for plane in range(PL):
         term = lax.dot_general(
-            parts[plane], faces[0, 0], (((1,), (1,)), ((), ())),
+            parts[plane], faces[0], (((1,), (1,)), ((), ())),
             precision=EXACT, preferred_element_type=F32,
         )
         beyond = beyond + jnp.where(lane_face % PL == plane, term, 0.0)
-    last = jnp.where(lane == VARS, jnp.full((GROUP * CAP, NK), links[0, 0], jnp.int32).astype(F32), 0.0)
+    slot = iota((GROUP * CAP, NK), 0)
+    first_lane = slot // (CAP * NZ) * (CAP * VARS) + slot % CAP * VARS
+    last = jnp.zeros((GROUP * CAP, NK), F32)
     for v in range(VARS):
         tail = jnp.sum(jnp.where(lane_face // PL == v, beyond, 0.0), axis=1, keepdims=True)
-        last = last + jnp.where(lane == v, a3 * tail, 0.0)
-    ends_out[...] = last.reshape(GROUP, CAP, NK)
-
-    def send_ends(i, carry):
-        py, pz = peer(i)
+        last = last + jnp.where(lane == first_lane + v, a3 * tail, 0.0)
+    owner_z = iota((NZ, GROUP * CAP), 1) // CAP % NZ
+    by_z = jnp.dot(
+        jnp.where(owner_z == iota((NZ, GROUP * CAP), 0), 1.0, 0.0), last,
+        precision=EXACT, preferred_element_type=F32,
+    )
+    donor = jnp.full((NZ, NK), links[0, 0], jnp.int32).astype(F32)
+    by_z = jnp.where(iota((NZ, NK), 1) == TAG, donor, by_z)
+    for plane in range(NZ):
+        ends_out[plane] = by_z[plane : plane + 1, :]
+
+    def send_ends(d, carry):
+        pz = (z + jnp.where(d % 2 == 1, NZ - d // 2, d // 2)) % NZ
         pltpu.make_async_remote_copy(
-            src_ref=ends_out.at[py * NZ + pz], dst_ref=ends_in.at[me],
-            send_sem=e_send, recv_sem=e_recv,
-            device_id={"gy": py, "gz": pz}, device_id_type=MESH,
+            src_ref=ends_out.at[pz], dst_ref=ends_in.at[y, z], send_sem=e_send, recv_sem=e_recv,
+            device_id={"gy": y, "gz": pz}, device_id_type=MESH,
         ).start()
         return carry
 
-    lax.fori_loop(0, GROUP - 1, send_ends, 0)
-    ends_in[me] = ends_out[me]
+    lax.fori_loop(0, NZ - 1, lambda i, c: send_ends(NZ - i, c), 0)
+    ends_in[y, z] = ends_out[z]
 
     lax.fori_loop(EARLY, GROUP - 1, send, 0)
     arrived[me] = sending[me]
 
+    others = pl.ds(0, GROUP - 1)
+    pltpu.make_async_copy(ends_out.at[in_line], ends_out.at[in_line], e_recv).wait()
+    forward = []
+    for s in range(1, NY):
+        forward.append(pltpu.make_async_remote_copy(
+            src_ref=ends_in.at[y], dst_ref=ends_in.at[y], send_sem=f_send.at[s], recv_sem=f_recv.at[s],
+            device_id={"gy": (y + s) % NY, "gz": z}, device_id_type=MESH,
+        ))
+        forward[-1].start()
     for copy in stage2:
         copy.wait()
 
     down = iota((NJ, NJ), 0)
     across = iota((NJ, NJ), 1)
-    for r, ghost, column in ((0, ghost_hi, 3), (1, ghost_lo, 1)):
-        layer = (got[0, r] + got[1, r]) + (got[2, r] + got[3, r])
+    layer = (got[0] + got[1]) + (got[2] + got[3])
+    for ghost, column in ((ghost_hi, 3), (ghost_lo, 1)):
         flipped = jnp.full((NJ, NJ), links[0, column], jnp.int32) == 1
         turn = jnp.where(across == jnp.where(flipped, NJ - 1 - down, down), 1.0, 0.0)
         ghost[...] = lax.dot_general(
@@ -315,7 +332,7 @@
                 for v in range(VARS)
             ]
             left = [
-                jnp.where(lane_k == 0, lo[:, v * PL + p : v * PL + p + 1], pltpu.roll(u[v], 1, 1))
+                jnp.where(lane_k == 0, lo[:, LAYER + v * PL + p : LAYER + v * PL + p + 1], pltpu.roll(u[v], 1, 1))
                 for v in range(VARS)
             ]
             after = face(mid, side(right, 2))
@@ -329,28 +346,32 @@
     put_state = pltpu.make_async_copy(state, state_out, out_sem.at[0])
     put_state.start()
 
-    others = pl.ds(0, GROUP - 1)
-    pltpu.make_async_copy(ends_in.at[others], ends_in.at[others], e_recv).wait()
+    for copy in forward:
+        copy.wait()
     for g in range(GROUP):
-        rows[pl.ds(CAP * g, CAP), pl.ds(0, NK)] = ends_in[g]
-    came = rows[:, pl.ds(0, NK)]
-    slot = iota((GROUP * CAP, GROUP * CAP), 0)
-    place = iota((GROUP * CAP, GROUP * CAP), 1)
-    donor_z = jnp.sum(jnp.where(slot == place, came[:, VARS : VARS + 1], 0.0), axis=0, keepdims=True)
-    home = place // (CAP * NZ) * (CAP * NZ) + place % CAP
-    move = jnp.where(slot.astype(F32) == home.astype(F32) + CAP * donor_z, 1.0, 0.0)
+        rows[pl.ds(g, 1), pl.ds(0, NK)] = ends_in[g // NZ, g % NZ]
+    came = rows[pl.ds(0, GROUP), pl.ds(0, NK)]
+    source = iota((GROUP, GROUP), 0)
+    place = iota((GROUP, GROUP), 1)
+    donor_z = jnp.sum(jnp.where(source == place, came[:, TAG : TAG + 1], 0.0), axis=0, keepdims=True)
+    donor = (place[0:1] // NZ * NZ).astype(F32) + donor_z
+    move = jnp.where((iota((GROUP * CAP, GROUP), 0) // CAP).astype(F32) == donor, 1.0, 0.0)
     gained = jnp.dot(move, came, precision=EXACT, preferred_element_type=F32)
+    mine = y * (CAP * VARS) + slot % CAP * VARS
+    tails = [
+        jnp.sum(jnp.where(lane == mine + v, gained, 0.0), axis=1, keepdims=True) for v in range(VARS)
+    ]
 
     pltpu.make_async_copy(arrived.at[others], arrived.at[others], m_recv).wait()
     for g in range(GROUP):
         fringe[pl.ds(CAP * g, CAP), :] = arrived[g]
     for v in range(VARS):
         here = fringe[:, pl.ds(v * NK, NK)]
-        fringe[:, pl.ds(v * NK, NK)] = here + jnp.where(lane == NK - 1, gained[:, v : v + 1], 0.0)
+        fringe[:, pl.ds(v * NK, NK)] = here + jnp.where(lane == NK - 1, tails[v], 0.0)
     put_fringe = pltpu.make_async_copy(fringe, fringe_out, out_sem.at[1])
     put_fringe.start()
     pltpu.make_async_copy(sending.at[others], sending.at[others], m_send).wait()
-    pltpu.make_async_copy(ends_out.at[others], ends_out.at[others], e_send).wait()
+    pltpu.make_async_copy(ends_out.at[in_line], ends_out.at[in_line], e_send).wait()
     pltpu.make_async_copy(notes.at[in_line], notes.at[in_line], n_send).wait()
     put_state.wait()
     put_fringe.wait()
@@ -391,18 +412,19 @@
             pltpu.VMEM((1, LINES), jnp.int32),
             pltpu.VMEM((3, 1, LINES), F32),
             pltpu.VMEM((1, LINES), jnp.int32),
-            pltpu.VMEM((QUAD, 2, FACE_ROWS, NJ), F32),
-            pltpu.VMEM((QUAD, 2, FACE_ROWS, NJ), F32),
-            pltpu.VMEM((QUAD, 2, FACE_ROWS, NJ), F32),
-            pltpu.VMEM((NJ, FACE_ROWS), F32),
-            pltpu.VMEM((NJ, FACE_ROWS), F32),
+            pltpu.VMEM((QUAD, 2 * LAYER, NJ), F32),
+            pltpu.VMEM((QUAD, 2 * LAYER, NJ), F32),
+            pltpu.VMEM((QUAD, 2 * LAYER, NJ), F32),
+            pltpu.VMEM((NJ, 2 * LAYER), F32),
+            pltpu.VMEM((NJ, 2 * LAYER), F32),
             pltpu.VMEM((GROUP, CAP, WIDE), F32),
             pltpu.VMEM((GROUP * CAP, PL * NJ), F32),
             pltpu.VMEM((GROUP * CAP, WIDE), F32),
             pltpu.VMEM((GROUP * CAP, NK), F32),
-            pltpu.VMEM((GROUP, CAP, NK), F32),
-            pltpu.VMEM((GROUP, CAP, NK), F32),
-            pltpu.VMEM((NZ, 4, 2 * LINES), F32),
+            pltpu.VMEM((NZ, 1, NK), F32),
+            pltpu.VMEM((NY, NZ, 1, NK), F32),
+            pltpu.VMEM((NZ, 3, 1, 2 * LINES), F32),
+            pltpu.VMEM((QUAD, 2, NJ), F32),
             pltpu.SemaphoreType.DMA((6,)),
             pltpu.SemaphoreType.DMA((QUAD,)),
             pltpu.SemaphoreType.DMA((QUAD,)),
@@ -414,6 +436,10 @@
             pltpu.SemaphoreType.DMA,
             pltpu.SemaphoreType.DMA,
             pltpu.SemaphoreType.DMA,
+            pltpu.SemaphoreType.DMA((QUAD,)),
+            pltpu.SemaphoreType.DMA((QUAD,)),
+            pltpu.SemaphoreType.DMA((NY,)),
+            pltpu.SemaphoreType.DMA((NY,)),
             pltpu.SemaphoreType.DMA((2,)),
         ],
         compiler_params=pltpu.CompilerParams(

time: 48.4 us -> 44.9 us (0.928)
  Pallas kernels: 47.3 us -> 44.1 us
    pallas_call x1, Pallas kernels: 45 us -> 41.9 us  [local(): pl.pallas_call(exchange_kernel, out_shape=(jax.ShapeDtypeStruct((VARS, PL...]
where the time goes in v3:
time: 44.9 us; the launch traced here: 44.8 us
  Pallas kernels  44.1 us (98%)
  between operations  0.64 us (1%)
    pallas_call x1, Pallas kernels, local(): pl.pallas_call(exchange_kernel, out_shape=(jax.ShapeDtypeStruct((VARS, PL...  41.9 us
    pallas_call x1, Pallas kernels, local(): pl.pallas_call(finish_kernel, out_shape=(jax.ShapeDtypeStruct((VARS, PL,...  2.23 us

profile of v3, /device:TPU:1, one launch (start us, length us, event | category | flops | bytes accessed | tf_op | source)
XLA Modules:
  0.0 44.8 jit_solution(6203683689783986562)
XLA Ops:
  0.6 41.9 %shard_map.77 = (f32[5,4,128,128]{3,2,1,0:T(8,128)}, f32[128,640]{1,0:T(8,128)}) custom-call(f32[5,4,128,128]{3,2,1,0:T(8,128)} %bitcast.10, s32[1,4]{1,0:T(1,128)} %bitcast.12, s32[1,64]{1,0:T(1,128)} %bitcast.13, s32[1,64]{1,0:T(1,128)} %bitcast.14, f32[3,1,64]{2,1,0:T(1,128)} %bitcast.11, s32[1,64]{1,0:T(1,128)} %bitcast.15), custom_call_target="tpu_custom_call" | custom-call | tf_op jit(solution)/shard_map/pallas_call | solution.py:397
  42.5 2.2 %shard_map.78 = (f32[5,4,128,128]{3,2,1,0:T(8,128)}, f32[128,640]{1,0:T(8,128)}) custom-call(f32[5,4,128,128]{3,2,1,0:T(8,128)} %get-tuple-element.6.state_in, f32[128,640]{1,0:T(8,128)} %get-tuple-element.7.fringe_in), custom_call_target="tpu_custom_call" | custom-call | tf_op jit(solution)/shard_map/pallas_call | solution.py:456

commit v4 on v3

--- a/solution.py
+++ b/solution.py
@@ -18,7 +18,7 @@
 WIDE = VARS * NK
 LAYER = VARS * PL
 F32 = jnp.float32
-ROOM = 60 * 1024 * 1024
+ROOM = 52 * 1024 * 1024
 
 
 def iota(shape, dim):
@@ -55,8 +55,8 @@
     return u, f, s
 
 
-def line_fields(dplane, dline, weights, owner):
-    own_row = owner[...].astype(F32)
+def line_fields(small):
+    own_row = small[0]
     earlier = iota((LINES, LINES), 0)
     later = iota((LINES, LINES), 1)
     own_col = jnp.sum(jnp.where(earlier == later, own_row, 0.0), axis=1, keepdims=True)
@@ -64,9 +64,7 @@
         jnp.where((own_col == own_row) & (earlier < later), 1.0, 0.0), axis=0, keepdims=True
     )
     slot_row = CAP * own_row + rank_row
-    return [
-        slot_row, dplane[...].astype(F32), dline[...].astype(F32), weights[0], weights[1], weights[2]
-    ]
+    return [slot_row] + [small[row] for row in range(1, 6)]
 
 
 def slot_matrix(fields, lane):
@@ -88,11 +86,11 @@
 
 
 def exchange_kernel(
-    flow, links_in, dplane_in, dline_in, weights_in, owner_in,
-    state_out, fringe_out,
-    state, arrived, fringe, cells, links, dplane, dline, weights, owner,
+    flow, small_in,
+    state, fringe,
+    arrived, cells, small,
     faces, chosen, got, ghost_lo, ghost_hi, sending, slots, rows, fracs, ends_out, ends_in, notes, tags,
-    in_sem, s1_send, s1_recv, s2_send, s2_recv, m_send, m_recv, e_send, e_recv, n_send, n_recv, t_send, t_recv, f_send, f_recv, out_sem,
+    in_sem, s1_send, s1_recv, s2_send, s2_recv, m_send, m_recv, e_send, e_recv, n_send, n_recv, t_send, t_recv, f_send, f_recv,
 ):
     y = lax.axis_index("gy")
     z = lax.axis_index("gz")
@@ -101,11 +99,7 @@
 
     loads = [
         pltpu.make_async_copy(flow, cells.at[:, :, pl.ds(PAD, NJ), :], in_sem.at[0]),
-        pltpu.make_async_copy(links_in, links, in_sem.at[1]),
-        pltpu.make_async_copy(dplane_in, dplane, in_sem.at[2]),
-        pltpu.make_async_copy(dline_in, dline, in_sem.at[3]),
-        pltpu.make_async_copy(weights_in, weights, in_sem.at[4]),
-        pltpu.make_async_copy(owner_in, owner, in_sem.at[5]),
+        pltpu.make_async_copy(small_in, small, in_sem.at[1]),
     ]
     for load in loads:
         load.start()
@@ -115,6 +109,9 @@
         dz = jnp.where(i % 2 == 0, d, NZ - d)
         dy = jnp.where(d == HALF, i, jnp.where(d == 0, i - 59, (i - 4) // 2))
         return (y + dy) % NY, (z + jnp.where(d == HALF, HALF, dz)) % NZ
+
+    def link(shape, column):
+        return jnp.broadcast_to(small[6, :, column : column + 1], shape)
 
     barrier = pltpu.get_barrier_semaphore()
 
@@ -142,10 +139,10 @@
             faces[0, pl.ds(v * PL + p, 1), :] = layer[0:1]
             faces[0, pl.ds(LAYER + v * PL + p, 1), :] = layer[1:2]
     for r in range(2):
-        tags[0, pl.ds(r, 1), :] = jnp.full((1, NJ), links[0, 2 * r], jnp.int32).astype(F32)
+        tags[0, pl.ds(r, 1), :] = link((1, NJ), 2 * r)
 
     lane = iota((GROUP * CAP, NK), 1)
-    fields = line_fields(dplane, dline, weights, owner)
+    fields = line_fields(small)
     lane_f = lane.astype(F32)
     parts, a3 = slot_matrix(fields, lane_f)
     for plane in range(PL):
@@ -251,14 +248,14 @@
             stage2[-1].start()
     in_line = pl.ds(0, NZ - 1)
     pltpu.make_async_copy(notes.at[in_line], notes.at[in_line], n_recv).wait()
-    below = jnp.full((1, 2 * LINES), links[0, 0], jnp.int32)
+    below = link((1, 2 * LINES), 0)
     theirs = []
     for row in range(3):
         wanted = jnp.zeros((1, 2 * LINES), F32)
         for source in range(NZ):
             wanted = wanted + jnp.where(below == source, notes[source, row], 0.0)
         theirs += [wanted[:, 0:LINES], wanted[:, LINES:]]
-    flipped = jnp.full((GROUP * CAP, NJ), links[0, 1], jnp.int32) == 1
+    flipped = link((GROUP * CAP, NJ), 1) == 1.0
     parts, a3 = slot_matrix(theirs, jnp.where(flipped, NJ - 1.0 - lane_f, lane_f))
     lane_face = iota((GROUP * CAP, 2 * LAYER), 1)
     beyond = jnp.zeros((GROUP * CAP, 2 * LAYER), F32)
@@ -279,7 +276,7 @@
         jnp.where(owner_z == iota((NZ, GROUP * CAP), 0), 1.0, 0.0), last,
         precision=EXACT, preferred_element_type=F32,
     )
-    donor = jnp.full((NZ, NK), links[0, 0], jnp.int32).astype(F32)
+    donor = link((NZ, NK), 0)
     by_z = jnp.where(iota((NZ, NK), 1) == TAG, donor, by_z)
     for plane in range(NZ):
         ends_out[plane] = by_z[plane : plane + 1, :]
@@ -314,7 +311,7 @@
     across = iota((NJ, NJ), 1)
     layer = (got[0] + got[1]) + (got[2] + got[3])
     for ghost, column in ((ghost_hi, 3), (ghost_lo, 1)):
-        flipped = jnp.full((NJ, NJ), links[0, column], jnp.int32) == 1
+        flipped = link((NJ, NJ), column) == 1.0
         turn = jnp.where(across == jnp.where(flipped, NJ - 1 - down, down), 1.0, 0.0)
         ghost[...] = lax.dot_general(
             turn, layer, (((1,), (1,)), ((), ())), precision=EXACT, preferred_element_type=F32
@@ -343,8 +340,6 @@
         return carry
 
     lax.fori_loop(0, NJ // 8, advance_k, 0)
-    put_state = pltpu.make_async_copy(state, state_out, out_sem.at[0])
-    put_state.start()
 
     for copy in forward:
         copy.wait()
@@ -368,50 +363,46 @@
     for v in range(VARS):
         here = fringe[:, pl.ds(v * NK, NK)]
         fringe[:, pl.ds(v * NK, NK)] = here + jnp.where(lane == NK - 1, tails[v], 0.0)
-    put_fringe = pltpu.make_async_copy(fringe, fringe_out, out_sem.at[1])
-    put_fringe.start()
     pltpu.make_async_copy(sending.at[others], sending.at[others], m_send).wait()
     pltpu.make_async_copy(ends_out.at[in_line], ends_out.at[in_line], e_send).wait()
     pltpu.make_async_copy(notes.at[in_line], notes.at[in_line], n_send).wait()
-    put_state.wait()
-    put_fringe.wait()
-
-
-def finish_kernel(state_in, fringe_in, state_out, fringe_out, state, fringe, in_sem, out_sem):
-    trips = [(fringe_in, fringe, fringe_out)]
-    for v in range(VARS):
-        trips.append((state_in.at[v], state.at[v], state_out.at[v]))
-    inward = [pltpu.make_async_copy(t[0], t[1], in_sem.at[i]) for i, t in enumerate(trips)]
-    outward = [pltpu.make_async_copy(t[1], t[2], out_sem.at[i]) for i, t in enumerate(trips)]
-    for copy in inward:
+
+
+def finish_kernel(state_in, fringe_in, state_out, fringe_out, sem):
+    copies = [pltpu.make_async_copy(fringe_in, fringe_out, sem.at[0])]
+    for v in range(VARS):
+        copies.append(pltpu.make_async_copy(state_in.at[v], state_out.at[v], sem.at[1 + v]))
+    for copy in copies:
         copy.start()
-    for first, second in zip(inward, outward):
-        first.wait()
-        second.start()
-    for copy in outward:
+    for copy in copies:
         copy.wait()
 
 
 def local(flow_state, face_links, donor_plane, donor_line, donor_weights, receptor_owner):
     anywhere = pl.BlockSpec(memory_space=pl.ANY)
+    vmem = pl.BlockSpec(memory_space=pltpu.VMEM)
+
+    def at(row, values):
+        after = 8 - row - values.shape[0]
+        beside = LINES - values.shape[2]
+        return jnp.pad(values, ((row, after), (0, 0), (0, beside)))
+
+    whole = at(0, receptor_owner.reshape(1, 1, LINES)) + at(1, donor_plane.reshape(1, 1, LINES))
+    whole = whole + at(2, donor_line.reshape(1, 1, LINES)) + at(6, face_links.reshape(1, 1, 4))
+    fractions = jnp.transpose(donor_weights, (0, 1, 4, 2, 3)).reshape(3, 1, LINES)
+    small = whole.astype(F32) + at(3, fractions)
     state, arrived = pl.pallas_call(
         exchange_kernel,
         out_shape=(
             jax.ShapeDtypeStruct((VARS, PL, NJ, NK), F32),
             jax.ShapeDtypeStruct((GROUP * CAP, WIDE), F32),
         ),
-        in_specs=[anywhere] * 6,
-        out_specs=(anywhere, anywhere),
+        in_specs=[anywhere] * 2,
+        out_specs=(vmem, vmem),
         scratch_shapes=[
-            pltpu.VMEM((VARS, PL, NJ, NK), F32),
             pltpu.VMEM((GROUP, CAP, WIDE), F32),
-            pltpu.VMEM((GROUP * CAP, WIDE), F32),
             pltpu.VMEM((VARS, PL, NJ + 2 * PAD, NK), F32),
-            pltpu.SMEM((1, 4), jnp.int32),
-            pltpu.VMEM((1, LINES), jnp.int32),
-            pltpu.VMEM((1, LINES), jnp.int32),
-            pltpu.VMEM((3, 1, LINES), F32),
-            pltpu.VMEM((1, LINES), jnp.int32),
+            pltpu.VMEM((8, 1, LINES), F32),
             pltpu.VMEM((QUAD, 2 * LAYER, NJ), F32),
             pltpu.VMEM((QUAD, 2 * LAYER, NJ), F32),
             pltpu.VMEM((QUAD, 2 * LAYER, NJ), F32),
@@ -425,7 +416,7 @@
             pltpu.VMEM((NY, NZ, 1, NK), F32),
             pltpu.VMEM((NZ, 3, 1, 2 * LINES), F32),
             pltpu.VMEM((QUAD, 2, NJ), F32),
-            pltpu.SemaphoreType.DMA((6,)),
+            pltpu.SemaphoreType.DMA((2,)),
             pltpu.SemaphoreType.DMA((QUAD,)),
             pltpu.SemaphoreType.DMA((QUAD,)),
             pltpu.SemaphoreType.DMA((QUAD,)),
@@ -440,18 +431,12 @@
             pltpu.SemaphoreType.DMA((QUAD,)),
             pltpu.SemaphoreType.DMA((NY,)),
             pltpu.SemaphoreType.DMA((NY,)),
-            pltpu.SemaphoreType.DMA((2,)),
         ],
         compiler_params=pltpu.CompilerParams(
             collective_id=0, has_side_effects=True, vmem_limit_bytes=ROOM
         ),
     )(
-        flow_state.reshape(VARS, PL, NJ, NK),
-        face_links.reshape(1, 4),
-        donor_plane.reshape(1, LINES),
-        donor_line.reshape(1, LINES),
-        jnp.transpose(donor_weights, (0, 1, 4, 2, 3)).reshape(3, 1, LINES),
-        receptor_owner.reshape(1, LINES),
+        flow_state.reshape(VARS, PL, NJ, NK), small
     )
     new_state, fringe = pl.pallas_call(
         finish_kernel,
@@ -461,13 +446,8 @@
         ),
         in_specs=[anywhere, anywhere],
         out_specs=(anywhere, anywhere),
-        scratch_shapes=[
-            pltpu.VMEM((VARS, PL, NJ, NK), F32),
-            pltpu.VMEM((GROUP * CAP, WIDE), F32),
-            pltpu.SemaphoreType.DMA((1 + VARS,)),
-            pltpu.SemaphoreType.DMA((1 + VARS,)),
-        ],
-        compiler_params=pltpu.CompilerParams(vmem_limit_bytes=ROOM),
+        scratch_shapes=[pltpu.SemaphoreType.DMA((1 + VARS,))],
+        compiler_params=pltpu.CompilerParams(vmem_limit_bytes=8 * 1024 * 1024),
     )(state, arrived)
     return (
         new_state.reshape(1, 1, 1, VARS, PL, NJ, NK),

time: 44.9 us -> 43.6 us (0.971)
  Pallas kernels: 44.1 us -> 42.1 us
  other arithmetic: 0 us -> 0.73 us
    pallas_call x1, Pallas kernels: 2.23 us -> 1.21 us  [local(): pl.pallas_call(finish_kernel, out_shape=(jax.ShapeDtypeStruct((VARS, PL,...]
    pallas_call x1, Pallas kernels: 41.9 us -> 40.9 us  [local(): pl.pallas_call(exchange_kernel, out_shape=(jax.ShapeDtypeStruct((VARS, PL...]
    add x0 -> x1, other arithmetic: none -> 0.73 us  [local(): small = whole.astype(F32) + at(3, fractions)]
where the time goes in v4:
time: 43.6 us; the launch traced here: 43.5 us
  Pallas kernels  42.1 us (97%)
  other arithmetic  0.73 us (2%)
  between operations  0.64 us (1%)
    pallas_call x1, Pallas kernels, local(): pl.pallas_call(exchange_kernel, out_shape=(jax.ShapeDtypeStruct((VARS, PL...  40.9 us
    pallas_call x1, Pallas kernels, local(): pl.pallas_call(finish_kernel, out_shape=(jax.ShapeDtypeStruct((VARS, PL,...  1.21 us

profile of v4, /device:TPU:1, one launch (start us, length us, event | category | flops | bytes accessed | tf_op | source)
XLA Modules:
  0.0 43.5 jit_solution(15859348592418239004)
XLA Ops:
  0.6 0.7 %pad_add_fusion.small_in = f32[8,1,64]{2,1,0:T(1,128)S(1)} fusion(f32[3,1,64]{2,1,0:T(1,128)} %bitcast.11, s32[1,1,4]{2,1,0:T(1,128)} %bitcast.12, s32[1,1,64]{2,1,0:T(1,128)} %bitcast.13, s32[1,1,64]{2,1,0:T(1,128)} %bitcast.14, s32[1,1,64]{2,1,0:T(1,128)} %bitcast.15), kind=kLoop, calls=%fused_computation | loop fusion | flops 2560 | bytes 3600 | tf_op jit(solution)/shard_map/add | solution.py:393
  1.4 40.9 %shard_map.77 = (f32[5,4,128,128]{3,2,1,0:T(8,128)S(1)}, f32[128,640]{1,0:T(8,128)S(1)}) custom-call(f32[5,4,128,128]{3,2,1,0:T(8,128)} %bitcast.10, f32[8,1,64]{2,1,0:T(1,128)S(1)} %pad_add_fusion.small_in), custom_call_target="tpu_custom_call" | custom-call | tf_op jit(solution)/shard_map/pallas_call | solution.py:394
  42.3 1.2 %shard_map.78 = (f32[5,4,128,128]{3,2,1,0:T(8,128)}, f32[128,640]{1,0:T(8,128)}) custom-call(f32[5,4,128,128]{3,2,1,0:T(8,128)S(1)} %get-tuple-element.6.state_in, f32[128,640]{1,0:T(8,128)S(1)} %get-tuple-element.7.fringe_in), custom_call_target="tpu_custom_call" | custom-call | tf_op jit(solution)/shard_map/pallas_call | solution.py:441
